TPU v7x, 32 devices: a whole 2x2x4 slice. The times are simulated.
32 devices in a mesh: groups: 2 (over y), pool: 16 (over z, x, core).
Axes of the slice: x: 2, y: 2, z: 4, core: 2. Of those that a mesh axis runs over, the one named last changes fastest.
Arguments:
- anchors: bfloat16 [4096, 1024], P(('groups', 'pool')), parts along dimension 0, may hold values from -7 to 7
- deltas: bfloat16 [4096, 15, 1024], P(('groups', 'pool')), parts along dimension 0, may hold values from -5 to 5
- scales: float32 [4096, 8], P(('groups', 'pool')), parts along dimension 0, may hold values from 0.15 to 0.8
- queries: bfloat16 [32, 8, 8192], P('groups'), parts along dimension 0, may hold values from -7 to 7
- lengths: int32 [32], P('groups'), parts along dimension 0, may hold values from 64 to 192, as said below
- page_owner: int32 [4096], P('groups'), parts along dimension 0, may hold values from 0 to 15, as said below
Outputs:
- decoded_cache: bfloat16 [4096, 16, 1024], P(('groups', 'pool')), parts along dimension 0
- attention: bfloat16 [32, 8, 8192], P('groups', None, 'pool'), parts along dimension 0
There are 2 independent parts, one for each index of `groups`. A program takes and returns all parts, laid end to end along the dimension named above; each array names one. Nothing has to cross between parts.
Inputs may be any that keep to these rules, and one draw needn't show every extreme that they name: `lengths`: pages of each request; together they cover all 2048 pages of the group. `page_owner`: each prefill device sends either none or exactly 16 of its pages to each decode device, and each decode device owns exactly 128 pages.
All inputs are finite; a program needn't handle non-finite values.
Results may differ from a plain program's by a relative error of at most 0.0046.
Values may be sent and summed in bfloat16 or wider, within the bound.
No kernel may reach another device: no remote copies, remote signals or barrier semaphores. Data moves between devices by JAX's collectives and lax.ppermute only.
A program may use at most 192 MiB of HBM per device.

v0:
```python
import functools
import jax
import jax.numpy as jnp
from jax import lax
from jax.experimental import pallas as pl
from jax.experimental.pallas import tpu as pltpu
from jax.sharding import PartitionSpec as P

QH = 64
KVH = 4
HD = 128
PAGE = 16
STEPS = 8
REQS = 16
KVW = 2 * KVH * HD
SPAN = 3
LOW = -1e30
VMEM_LIMIT = 48 * 1024 * 1024
F32 = jnp.float32
BF16 = jnp.bfloat16
I32 = jnp.int32


def decode_kernel(chunk, place, flags, blocks, anchors, deltas, scales, out, rows, staged, sems):
    step = pl.program_id(0)
    for head in range(2 * KVH):
        cols = slice(head * HD, (head + 1) * HD)
        scale = jnp.broadcast_to(scales[:, head : head + 1], (chunk, HD))
        anchor = anchors[:, cols].astype(F32)
        rows[head * PAGE * chunk : head * PAGE * chunk + chunk, :] = anchor
        for token in range(1, PAGE):
            start = (head * PAGE + token) * chunk
            rows[start : start + chunk, :] = anchor + scale * deltas[token - 1, :, cols].astype(F32)
    for page in range(chunk):
        picked = [
            rows[pl.ds(head * PAGE * chunk + page, PAGE, stride=chunk), :]
            for head in range(2 * KVH)
        ]
        staged[place[step * chunk + page]] = jnp.concatenate(picked, axis=1).astype(BF16)

    @pl.when(step == pl.num_programs(0) - 1)
    def flush():
        copies = []
        for owner in range(16):
            copy = pltpu.make_async_copy(
                staged.at[pl.ds(blocks[owner] * PAGE, PAGE)],
                out.at[pl.ds(owner * PAGE, PAGE)],
                sems.at[owner],
            )
            pl.when(flags[owner] > 0)(copy.start)
            copies.append(copy)
        for owner in range(16):
            pl.when(flags[owner] > 0)(copies[owner].wait)


def decode_sorted(place, flags, blocks, anchors, deltas, scales):
    number = anchors.shape[0]
    chunk = 16
    return pl.pallas_call(
        functools.partial(decode_kernel, chunk),
        grid_spec=pltpu.PrefetchScalarGridSpec(
            num_scalar_prefetch=3,
            grid=(number // chunk,),
            in_specs=[
                pl.BlockSpec((chunk, KVW), lambda i, *_: (i, 0)),
                pl.BlockSpec((PAGE - 1, chunk, KVW), lambda i, *_: (0, i, 0)),
                pl.BlockSpec((chunk, 2 * KVH), lambda i, *_: (i, 0)),
            ],
            out_specs=pl.BlockSpec(memory_space=pl.ANY),
            scratch_shapes=[
                pltpu.VMEM((2 * KVH * PAGE * chunk, HD), F32),
                pltpu.VMEM((number, PAGE, KVW), BF16),
                pltpu.SemaphoreType.DMA((16,)),
            ],
        ),
        out_shape=jax.ShapeDtypeStruct((16 * PAGE, PAGE, KVW), BF16),
        compiler_params=pltpu.CompilerParams(vmem_limit_bytes=VMEM_LIMIT),
        name="decode_sorted",
    )(place, flags, blocks, anchors, deltas, scales)


def attend_kernel(plan, requests, first, second, third, key_anchor, val_anchor, key_delta, val_delta, scales, after, out, keys, vals):
    head = pl.program_id(0)
    number = key_anchor.shape[0]
    table = jnp.transpose(scales[...])
    lane = lax.broadcasted_iota(I32, table.shape, 1)
    key_scale = jnp.sum(jnp.where(lane == head, table, 0.0), axis=1, keepdims=True)
    val_scale = jnp.sum(jnp.where(lane == head + KVH, table, 0.0), axis=1, keepdims=True)
    for anchor, delta, scale, kept in (
        (key_anchor, key_delta, key_scale, keys),
        (val_anchor, val_delta, val_scale, vals),
    ):
        kept[0:number, :] = anchor[...]
        wide = anchor[...].astype(F32)
        for token in range(1, PAGE):
            kept[token * number : (token + 1) * number, :] = (
                wide + scale * delta[token - 1].astype(F32)
            ).astype(BF16)
    token_request = jnp.concatenate([requests[4:5, :]] * PAGE, axis=1) - plan[5, 0]
    rows = STEPS * QH // KVH
    eye = lax.broadcasted_iota(I32, (rows, rows), 0) == lax.broadcasted_iota(I32, (rows, rows), 1)
    pieces = []
    for slot, queries in enumerate((first, second, third)):
        wide = queries[0].astype(F32)
        picked = jnp.concatenate(
            [wide[:, group * HD : (group + 1) * HD] for group in range(QH // KVH)], axis=0
        ).astype(BF16)
        scores = lax.dot_general(
            picked, keys[...], (((1,), (1,)), ((), ())), preferred_element_type=F32
        ) * HD ** (-0.5)
        inside = token_request == slot
        scores = jnp.where(inside, scores, LOW)
        top = jnp.max(scores, axis=1, keepdims=True)
        exponent = jnp.where(inside, jnp.exp(scores - top), 0.0)
        total = jnp.maximum(jnp.sum(exponent, axis=1, keepdims=True), 1e-30)
        numer = jnp.dot(exponent.astype(BF16), vals[...], preferred_element_type=F32)
        mean = (numer * (1.0 / total)).astype(BF16)
        quarter = rows // 4
        for part in range(4):
            out[part, slot * quarter : (slot + 1) * quarter, :] = mean[
                part * quarter : (part + 1) * quarter
            ]
        level = top + jnp.log(total)
        line = jnp.sum(jnp.where(eye, level, 0.0), axis=0, keepdims=True)
        for _ in range(3):
            piece = line.astype(BF16).astype(F32)
            pieces.append(piece)
            line = line - piece
    pieces.append(jnp.zeros((16 - len(pieces), rows), F32))
    stats = jnp.concatenate(pieces, axis=0).astype(BF16)
    for part in range(4):
        out[part, 96:112, :] = stats


def attend(plan, queries, anchors, deltas, scales, after):
    number = anchors.shape[0]
    rows = STEPS * QH // KVH
    return pl.pallas_call(
        attend_kernel,
        grid_spec=pltpu.PrefetchScalarGridSpec(
            num_scalar_prefetch=1,
            grid=(KVH,),
            in_specs=[
                pl.BlockSpec((8, number), lambda h, *_: (0, 0)),
                *[
                    pl.BlockSpec((1, STEPS, rows * HD // STEPS), lambda h, p, k=k: (p[5, 0] + k, 0, h))
                    for k in range(SPAN)
                ],
                pl.BlockSpec((number, HD), lambda h, *_: (0, h)),
                pl.BlockSpec((number, HD), lambda h, *_: (0, h + KVH)),
                pl.BlockSpec((PAGE - 1, number, HD), lambda h, *_: (0, 0, h)),
                pl.BlockSpec((PAGE - 1, number, HD), lambda h, *_: (0, 0, h + KVH)),
                pl.BlockSpec((2 * KVH, number), lambda h, *_: (0, 0)),
                pl.BlockSpec(memory_space=pl.ANY),
            ],
            out_specs=pl.BlockSpec((4, 112, HD), lambda h, *_: (h, 0, 0)),
            scratch_shapes=[
                pltpu.VMEM((PAGE * number, HD), BF16),
                pltpu.VMEM((PAGE * number, HD), BF16),
            ],
        ),
        out_shape=jax.ShapeDtypeStruct((16, 112, HD), BF16),
        compiler_params=pltpu.CompilerParams(vmem_limit_bytes=VMEM_LIMIT),
        name="attend",
    )(plan, plan, queries, queries, queries, anchors, anchors, deltas, deltas, scales, after)


def merge_kernel(plan, place, parts, out, level, top, total, numer):
    quarter = 32
    row = lax.broadcasted_iota(I32, (quarter, HD), 0)
    lane = lax.broadcasted_iota(I32, (quarter, HD), 1)
    mine = lane == row + quarter * ((place[0] & 1) * 2 + place[1])
    top[...] = jnp.full(top.shape, LOW, F32)
    total[...] = jnp.zeros(total.shape, F32)
    numer[...] = jnp.zeros(numer.shape, F32)
    for sender in range(16):
        stats = parts[sender, 96:112, :].astype(F32)
        for slot in range(SPAN):
            line = stats[3 * slot : 3 * slot + 1] + (
                stats[3 * slot + 1 : 3 * slot + 2] + stats[3 * slot + 2 : 3 * slot + 3]
            )
            column = jnp.sum(jnp.where(mine, line, 0.0), axis=1, keepdims=True)
            column = jnp.broadcast_to(column, (quarter, HD))
            level[sender * SPAN + slot] = column
            request = plan[3, sender] + slot
            top[request] = jnp.maximum(top[request], column)
    for sender in range(16):
        for slot in range(SPAN):
            request = plan[3, sender] + slot
            weight = jnp.exp(level[sender * SPAN + slot] - top[request])
            mean = parts[sender, slot * quarter : (slot + 1) * quarter, :].astype(F32)
            total[request] += weight
            numer[request] += weight * mean
    for request in range(REQS):
        result = (numer[request] / total[request]).astype(BF16)
        for group in range(4):
            out[request, :, group * HD : (group + 1) * HD] = result[
                group * STEPS : (group + 1) * STEPS
            ]


def merge(plan, place, parts):
    return pl.pallas_call(
        merge_kernel,
        grid_spec=pltpu.PrefetchScalarGridSpec(
            num_scalar_prefetch=2,
            grid=(1,),
            in_specs=[pl.BlockSpec((16, 112, HD), lambda i, *_: (0, 0, 0))],
            out_specs=pl.BlockSpec((REQS, STEPS, 4 * HD), lambda i, *_: (0, 0, 0)),
            scratch_shapes=[
                pltpu.VMEM((16 * SPAN, 32, HD), F32),
                pltpu.VMEM((REQS, 32, HD), F32),
                pltpu.VMEM((REQS, 32, HD), F32),
                pltpu.VMEM((REQS, 32, HD), F32),
            ],
        ),
        out_shape=jax.ShapeDtypeStruct((REQS, STEPS, 4 * HD), BF16),
        compiler_params=pltpu.CompilerParams(vmem_limit_bytes=VMEM_LIMIT),
        name="merge",
    )(plan, place, parts)


def assemble_kernel(flags, blocks, arrived, out, staged, in_sems, out_sems):
    reads, writes = [], []
    for sender in range(16):
        rows = pl.ds(blocks[sender] * PAGE, PAGE)
        source = arrived.at[pl.ds(sender * PAGE, PAGE)]
        reads.append(pltpu.make_async_copy(source, staged.at[rows], in_sems.at[sender]))
        writes.append(pltpu.make_async_copy(staged.at[rows], out.at[rows], out_sems.at[sender]))
    for sender in range(16):
        pl.when(flags[sender] > 0)(reads[sender].start)
    for sender in range(16):

        @pl.when(flags[sender] > 0)
        def forward():
            reads[sender].wait()
            writes[sender].start()

    for sender in range(16):
        pl.when(flags[sender] > 0)(writes[sender].wait)


def assemble(flags, blocks, arrived, number):
    return pl.pallas_call(
        assemble_kernel,
        grid_spec=pltpu.PrefetchScalarGridSpec(
            num_scalar_prefetch=2,
            grid=(1,),
            in_specs=[pl.BlockSpec(memory_space=pl.ANY)],
            out_specs=pl.BlockSpec(memory_space=pl.ANY),
            scratch_shapes=[
                pltpu.VMEM((number, PAGE, KVW), BF16),
                pltpu.SemaphoreType.DMA((16,)),
                pltpu.SemaphoreType.DMA((16,)),
            ],
        ),
        out_shape=jax.ShapeDtypeStruct((number, PAGE, KVW), BF16),
        compiler_params=pltpu.CompilerParams(vmem_limit_bytes=VMEM_LIMIT),
        name="assemble",
    )(flags, blocks, arrived)


ROUNDS = 9
LIMIT = 12
UNIT = 2
LAG = 2
SIDE_LAG = 3
SLOTS = 7
HALF = PAGE // 2
FAR = 1e6


def units_of(port, time):
    if port < 2:
        return UNIT
    if time >= 8:
        return 2
    return 3 if time in (0, 2, 4, 6, 7) else 0


def plan_kernel(place, lengths, owners, out):
    chip = place[0]
    row = lax.broadcasted_iota(I32, (16, 128), 0)
    lanes = lax.broadcasted_iota(I32, (16, 128), 1)
    sender_of = lanes >> 3
    turn = (lanes & 7).astype(F32)
    table = owners[...]
    running = jnp.zeros((16, 1), F32)
    sends = []
    targets = jnp.zeros((16, 128), F32)
    for owner in range(16):
        flag = jnp.max(jnp.where(table == owner, 1.0, 0.0), axis=1, keepdims=True)
        targets += jnp.where(turn == running, flag * owner, 0.0)
        sends.append(flag)
        running = running + flag
    dest = jnp.sum(jnp.where(row == sender_of, targets, 0.0), axis=0, keepdims=True)
    hits = jnp.zeros((16, 128), F32)
    for owner in range(16):
        hits += sends[owner] * jnp.where(dest == owner, 1.0, 0.0)
    rank = jnp.sum(jnp.where(row < sender_of, hits, 0.0), axis=0, keepdims=True).astype(I32)
    dest = dest.astype(I32)
    lane = lax.broadcasted_iota(I32, (1, 128), 1)
    sender = lane >> 3
    from_z, from_x = sender >> 2, (sender >> 1) & 1
    to_z, to_x = dest >> 2, (dest >> 1) & 1
    crosses = (from_z >> 1) != (to_z >> 1)
    below = jnp.where(
        lax.broadcasted_iota(I32, (128, 128), 0) < lax.broadcasted_iota(I32, (128, 128), 1), 1.0, 0.0
    )
    line = from_x
    for side in range(2):
        leaving = crosses & ((from_z >> 1) == side)
        free = jnp.where(leaving & (from_x != to_x), 1.0, 0.0)
        fixed = jnp.where(leaving & (from_x == to_x), 1.0, 0.0)
        tilt = jnp.sum(fixed * (2 * from_x - 1).astype(F32), axis=1, keepdims=True)
        count = jnp.sum(free, axis=1, keepdims=True)
        share = jnp.clip(jnp.floor((tilt + count) * 0.5), 0.0, count)
        step = share / jnp.maximum(count, 1.0)
        index = jnp.dot(jnp.broadcast_to(free, (8, 128)), below, preferred_element_type=F32)[0:1]
        first = jnp.floor((index + 1.0) * step + 1e-3) > jnp.floor(index * step + 1e-3)
        line = jnp.where(free > 0.0, jnp.where(first, 0, 1), line)
    chips = lax.broadcasted_iota(I32, (8, 128), 0)
    mine = lax.broadcasted_iota(I32, (8, 1), 0) == chip

    def round_step(time, carry):
        at_z, at_x, ready, code, steps, needed = carry
        waits = crosses & ((at_z >> 1) == (from_z >> 1))
        turns = ((at_z == to_z) & (at_x != to_x)) | (waits & (line != at_x))
        along = jnp.logical_not(turns) & (at_z != to_z)
        left = jnp.abs(to_z - at_z) + jnp.where(at_x != to_x, 1, 0)
        key = ((8 - left) * 128 + lane).astype(F32)
        here = (at_z * 2 + at_x == chips) & (ready <= time)
        heading = jnp.where(turns, 2, jnp.where(along, jnp.where(to_z > at_z, 0, 1), 3))
        moved = jnp.zeros((1, 128), F32)
        landed = jnp.zeros((1, 128), F32)
        value = (code + 1).astype(F32)
        side = sum(jnp.where(time == t, units_of(2, t), 0) for t in range(LIMIT))
        for port in range(3):
            keys = jnp.where(here & (heading == port), key, FAR)
            for unit in range(UNIT if port < 2 else 3):
                if port == 2:
                    keys = jnp.where(unit < side, keys, FAR)
                least = jnp.min(keys, axis=1, keepdims=True)
                chosen = jnp.where((keys == least) & (keys < FAR), 1.0, 0.0)
                source = jnp.sum(chosen * value, axis=1, keepdims=True)
                source = jnp.sum(jnp.where(mine, source, 0.0), axis=0, keepdims=True)
                slot = SLOTS * time + UNIT * port + unit
                steps = steps + jnp.where(lane == slot, source, 0.0)
                taken = jnp.sum(chosen, axis=0, keepdims=True)
                moved = moved + taken * (port + 1)
                landed = landed + taken * (slot + 16).astype(F32)
                keys = jnp.where(chosen > 0.0, FAR, keys)
        went = moved.astype(I32)
        at_z = at_z + jnp.where(went == 1, 1, 0) - jnp.where(went == 2, 1, 0)
        at_x = jnp.where(went == 3, 1 - at_x, at_x)
        ready = jnp.where(went > 0, time + jnp.where(went == 3, SIDE_LAG, LAG), ready)
        code = jnp.where(went > 0, landed.astype(I32), code)
        any_move = jnp.max(moved, axis=1, keepdims=True)
        needed = jnp.where(any_move > 0.0, (time + 1).astype(F32), needed)
        return at_z, at_x, ready, code, steps, needed

    start = (
        from_z,
        from_x,
        jnp.zeros((1, 128), I32),
        (sender & 1) * 8 + (lane & 7),
        jnp.zeros((1, 128), F32),
        jnp.zeros((1, 1), F32),
    )
    at_z, at_x, ready, code, steps, needed = lax.fori_loop(0, LIMIT, round_step, start)
    undone = jnp.where((at_z == to_z) & (at_x == to_x), 0.0, 1.0)
    undone = jnp.max(undone, axis=1, keepdims=True)
    needed = jnp.where(undone > 0.0, float(LIMIT + 1), needed)
    arrives = (dest >> 1) == chip
    slots = (dest & 1) * 8 + rank
    final = jnp.sum(
        jnp.where((row == slots) & arrives, (code + 1).astype(F32), 0.0), axis=1, keepdims=True
    )
    final = jnp.sum(jnp.where(row == lanes, final, 0.0), axis=0, keepdims=True)
    out[0:1, :] = steps.astype(I32)
    out[1:2, :] = final.astype(I32)
    out[2:3, :] = jnp.broadcast_to(needed, (1, 128)).astype(I32)
    page = (2 * chip + place[1]) * 128 + lane
    requests = jnp.zeros((1, 128), I32)
    bases = jnp.zeros((1, 128), I32)
    end = 0
    for request in range(REQS):
        end = end + lengths[request]
        requests = requests + jnp.where(page >= end, 1, 0)
        bases = bases + jnp.where(lane * 128 >= end, 1, 0)
    bases = jnp.minimum(bases, REQS - SPAN)
    base = jnp.sum(jnp.where(lane == 2 * chip + place[1], bases, 0).astype(F32), axis=1, keepdims=True)
    out[3:4, :] = bases
    out[4:5, :] = requests
    out[5:6, :] = jnp.broadcast_to(base, (1, 128)).astype(I32)
    out[6:8, :] = jnp.zeros((2, 128), I32)


def make_plan(place, lengths, page_owner):
    return pl.pallas_call(
        plan_kernel,
        grid_spec=pltpu.PrefetchScalarGridSpec(
            num_scalar_prefetch=2,
            grid=(1,),
            in_specs=[pl.BlockSpec((16, 128), lambda i, *_: (0, 0))],
            out_specs=pl.BlockSpec((8, 128), lambda i, *_: (0, 0)),
        ),
        out_shape=jax.ShapeDtypeStruct((8, 128), I32),
        name="make_plan",
    )(place, lengths, page_owner.reshape(16, 128))


def halves_kernel(place, owners, anchors, deltas, scales, keep, give, swap, columns, ranks, order, rows, staged, sems):
    step = pl.program_id(0)
    count = PAGE * PAGE

    @pl.when(step == 0)
    def build():
        row = lax.broadcasted_iota(I32, (count, count), 0)
        lane = lax.broadcasted_iota(I32, (count, count), 1)
        swap[...] = jnp.where(lane == (row & 15) * PAGE + (row >> 4), 1.0, 0.0).astype(BF16)
        columns[...] = jnp.transpose(scales[...])
        number = owners.shape[1]
        row = lax.broadcasted_iota(I32, (number, number), 0)
        lane = lax.broadcasted_iota(I32, (number, number), 1)
        across = owners[pl.ds(2 * place[0] + place[1], 1), :].astype(F32)
        down = jnp.sum(jnp.where(row == lane, across, 0.0), axis=1, keepdims=True)
        ahead = (down < across) | ((down == across) & (row < lane))
        ranks[...] = jnp.sum(jnp.where(ahead, 1.0, 0.0), axis=0, keepdims=True).astype(I32)
        pltpu.make_async_copy(ranks, order, sems.at[2]).start()

    core = place[1]
    for part in range(anchors.shape[0] // PAGE):
        pages = slice(part * PAGE, (part + 1) * PAGE)
        for head in range(2 * KVH):
            cols = slice(head * HD, (head + 1) * HD)
            start = pl.multiple_of(step * anchors.shape[0] + part * PAGE, PAGE)
            scale = jnp.broadcast_to(columns[pl.ds(start, PAGE), head : head + 1], (PAGE, HD))
            first = anchors[pages, cols]
            anchor = first.astype(F32)
            rows[0:PAGE, cols] = first
            for token in range(1, PAGE):
                rebuilt = anchor + scale * deltas[token - 1, pages, cols].astype(F32)
                rows[token * PAGE : (token + 1) * PAGE, cols] = rebuilt.astype(BF16)
        turned = jnp.dot(swap[...], rows[...], preferred_element_type=F32).astype(BF16)
        if part == 0:

            @pl.when(step == 0)
            def ordered():
                pltpu.make_async_copy(ranks, order, sems.at[2]).wait()

        for page in range(PAGE):
            rank = order[0, step * anchors.shape[0] + part * PAGE + page]
            half = (rank >> 3) & 1
            slot = (half ^ core) * 64 + (rank >> 4) * HALF + (rank & 7)
            staged[slot] = turned[page * PAGE : (page + 1) * PAGE]

    @pl.when(step == pl.num_programs(0) - 1)
    def flush():
        copies = [
            pltpu.make_async_copy(staged.at[pl.ds(64, 64)], give, sems.at[0]),
            pltpu.make_async_copy(staged.at[pl.ds(0, 64)], keep, sems.at[1]),
        ]
        for copy in copies:
            copy.start()
        for copy in copies:
            copy.wait()


def decode_halves(place, page_owner, anchors, deltas, scales):
    number = anchors.shape[0]
    chunk = 2 * PAGE
    half = jax.ShapeDtypeStruct((number // 2, PAGE, KVW), BF16)
    return pl.pallas_call(
        halves_kernel,
        grid_spec=pltpu.PrefetchScalarGridSpec(
            num_scalar_prefetch=1,
            grid=(number // chunk,),
            in_specs=[
                pl.BlockSpec((16, number), lambda i, *_: (0, 0)),
                pl.BlockSpec((chunk, KVW), lambda i, *_: (i, 0)),
                pl.BlockSpec((PAGE - 1, chunk, KVW), lambda i, *_: (0, i, 0)),
                pl.BlockSpec((2 * KVH, number), lambda i, *_: (0, 0)),
            ],
            out_specs=[pl.BlockSpec(memory_space=pl.ANY)] * 2,
            scratch_shapes=[
                pltpu.VMEM((PAGE * PAGE, PAGE * PAGE), BF16),
                pltpu.VMEM((number, 2 * KVH), F32),
                pltpu.VMEM((1, number), I32),
                pltpu.SMEM((1, number), I32),
                pltpu.VMEM((PAGE * PAGE, KVW), BF16),
                pltpu.VMEM((number, PAGE, KVW), BF16),
                pltpu.SemaphoreType.DMA((3,)),
            ],
        ),
        out_shape=(half, half),
        compiler_params=pltpu.CompilerParams(vmem_limit_bytes=VMEM_LIMIT),
        name="decode_halves",
    )(place, page_owner.reshape(16, number), anchors, deltas, scales)


def fetch(code, core, own, landed, ports, target, sem):
    value = code - 1
    keep, got = own

    @pl.when((value >= 0) & (value < 16))
    def from_own():
        rows = pl.ds((value & 7) * HALF, HALF)

        @pl.when((value >> 3) == core)
        def kept():
            pltpu.make_async_copy(keep.at[rows], target, sem).start()

        @pl.when((value >> 3) != core)
        def gotten():
            pltpu.make_async_copy(got.at[rows], target, sem).start()

    for time, port, arrivals in landed:
        if port in ports:
            offset = value - 16 - SLOTS * time - UNIT * port

            @pl.when((offset >= 0) & (offset < units_of(port, time)))
            def from_round():
                rows = pl.ds(offset * HALF, HALF)
                pltpu.make_async_copy(arrivals.at[rows], target, sem).start()


def settle(code, own, target, sem):
    @pl.when(code > 0)
    def wait():
        pltpu.make_async_copy(own[0].at[pl.ds(0, HALF)], target, sem).wait()


def pick_kernel(time, tags, plan, place, *refs):
    own, landed = refs[:2], [tag + (ref,) for tag, ref in zip(tags, refs[2:])]
    used = [port for port in range(3) if units_of(port, time)]
    outs, sems = refs[-1 - len(used) : -1], refs[-1]
    for phase in range(2):
        for port, out in zip(used, outs):
            ports = (0, 1) if port == 2 else (port, 2)
            for unit in range(units_of(port, time)):
                code = plan[0, SLOTS * time + UNIT * port + unit]
                target = out.at[pl.ds(unit * HALF, HALF)]
                sem = sems.at[UNIT * port + unit]
                if phase == 0:
                    fetch(code, place[1], own, landed, ports, target, sem)
                else:
                    settle(code, own, target, sem)


def pick(time, plan, place, own, landed, after):
    landed = [item for item in landed if item[0] + (SIDE_LAG if item[1] == 2 else LAG) <= time]
    sources = list(own) + [item[2] for item in landed] + [after]
    pieces = [
        jax.ShapeDtypeStruct((units_of(port, time) * HALF, PAGE, KVW), BF16)
        for port in range(3)
        if units_of(port, time)
    ]
    return pl.pallas_call(
        functools.partial(pick_kernel, time, [item[:2] for item in landed]),
        grid_spec=pltpu.PrefetchScalarGridSpec(
            num_scalar_prefetch=2,
            grid=(1,),
            in_specs=[pl.BlockSpec(memory_space=pl.ANY)] * len(sources),
            out_specs=[pl.BlockSpec(piece.shape, lambda i, *_: (0, 0, 0)) for piece in pieces],
            scratch_shapes=[pltpu.SemaphoreType.DMA((SLOTS,))],
        ),
        out_shape=pieces,
        compiler_params=pltpu.CompilerParams(vmem_limit_bytes=VMEM_LIMIT),
        name=f"pick_{time}",
    )(plan, place, *sources)


def give_kernel(tags, plan, place, *refs):
    own, landed = refs[:2], [tag + (ref,) for tag, ref in zip(tags, refs[2:])]
    out, sems = refs[-2:]
    core = place[1]
    codes = [plan[1, (1 - core) * 8 + slot] for slot in range(8)]
    targets = [out.at[pl.ds(slot * HALF, HALF)] for slot in range(8)]
    for slot in range(8):
        fetch(codes[slot], core, own, landed, (0, 1, 2), targets[slot], sems.at[slot])
    for slot in range(8):
        settle(codes[slot], own, targets[slot], sems.at[slot])


def gather_give(plan, place, own, landed, after):
    sources = list(own) + [item[2] for item in landed] + [after]
    shape = (8 * HALF, PAGE, KVW)
    return pl.pallas_call(
        functools.partial(give_kernel, [item[:2] for item in landed]),
        grid_spec=pltpu.PrefetchScalarGridSpec(
            num_scalar_prefetch=2,
            grid=(1,),
            in_specs=[pl.BlockSpec(memory_space=pl.ANY)] * len(sources),
            out_specs=pl.BlockSpec(shape, lambda i, *_: (0, 0, 0)),
            scratch_shapes=[pltpu.SemaphoreType.DMA((8,))],
        ),
        out_shape=jax.ShapeDtypeStruct(shape, BF16),
        compiler_params=pltpu.CompilerParams(vmem_limit_bytes=VMEM_LIMIT),
        name="gather_give",
    )(plan, place, *sources)


def own_kernel(tags, plan, place, *refs):
    own, landed = refs[:2], [tag + (ref,) for tag, ref in zip(tags, refs[2:])]
    out, staged, in_sems, out_sems = refs[-4:]
    core = place[1]
    codes = [plan[1, core * 8 + slot] for slot in range(8)]
    targets = [staged.at[pl.ds(slot * HALF, HALF)] for slot in range(8)]
    for slot in range(8):
        fetch(codes[slot], core, own, landed, (0, 1, 2), targets[slot], in_sems.at[slot])
    writes = []
    for slot in range(8):
        start = slot * PAGE + core * HALF
        writes.append(
            pltpu.make_async_copy(targets[slot], out.at[pl.ds(start, HALF)], out_sems.at[slot])
        )
        settle(codes[slot], own, targets[slot], in_sems.at[slot])
        writes[slot].start()
    for write in writes:
        write.wait()


def gather_own(plan, place, own, landed):
    sources = list(own) + [item[2] for item in landed]
    return pl.pallas_call(
        functools.partial(own_kernel, [item[:2] for item in landed]),
        grid_spec=pltpu.PrefetchScalarGridSpec(
            num_scalar_prefetch=2,
            grid=(1,),
            in_specs=[pl.BlockSpec(memory_space=pl.ANY)] * len(sources),
            out_specs=pl.BlockSpec(memory_space=pl.ANY),
            scratch_shapes=[
                pltpu.VMEM((8 * HALF, PAGE, KVW), BF16),
                pltpu.SemaphoreType.DMA((8,)),
                pltpu.SemaphoreType.DMA((8,)),
            ],
        ),
        out_shape=jax.ShapeDtypeStruct((8 * PAGE, PAGE, KVW), BF16),
        compiler_params=pltpu.CompilerParams(vmem_limit_bytes=VMEM_LIMIT),
        name="gather_own",
    )(plan, place, *sources)


def fill_kernel(place, cache, other, out, staged, in_sems, out_sems):
    half = 1 - place[1]
    reads, writes = [], []
    for slot in range(8):
        rows = pl.ds(slot * HALF, HALF)
        reads.append(pltpu.make_async_copy(other.at[rows], staged.at[rows], in_sems.at[slot]))
        writes.append(
            pltpu.make_async_copy(
                staged.at[rows], out.at[pl.ds(slot * PAGE + half * HALF, HALF)], out_sems.at[slot]
            )
        )
    for read in reads:
        read.start()
    for read, write in zip(reads, writes):
        read.wait()
        write.start()
    for write in writes:
        write.wait()


def fill(place, cache, other):
    return pl.pallas_call(
        fill_kernel,
        grid_spec=pltpu.PrefetchScalarGridSpec(
            num_scalar_prefetch=1,
            grid=(1,),
            in_specs=[pl.BlockSpec(memory_space=pl.ANY)] * 2,
            out_specs=pl.BlockSpec(memory_space=pl.ANY),
            scratch_shapes=[
                pltpu.VMEM((8 * HALF, PAGE, KVW), BF16),
                pltpu.SemaphoreType.DMA((8,)),
                pltpu.SemaphoreType.DMA((8,)),
            ],
        ),
        out_shape=jax.ShapeDtypeStruct(cache.shape, cache.dtype),
        input_output_aliases={1: 0},
        compiler_params=pltpu.CompilerParams(vmem_limit_bytes=VMEM_LIMIT),
        name="fill",
    )(place, cache, other)


UP = tuple((i, i + 4) for i in range(12))
DOWN = tuple((i + 4, i) for i in range(12))
ACROSS = tuple((i, i ^ 2) for i in range(16))
TWIN = tuple((i, i ^ 1) for i in range(16))


def ship(time, parts):
    used = [port for port in range(3) if units_of(port, time)]
    hops = (UP, DOWN, ACROSS)
    return [(time, port, lax.ppermute(part, "pool", hops[port])) for port, part in zip(used, parts)]


def finish(plan, place, own, landed, after):
    other = lax.ppermute(gather_give(plan, place, own, landed, after), "pool", TWIN)
    return fill(place, gather_own(plan, place, own, landed), other)


def local_lanes(anchors, deltas, scales, queries, lengths, page_owner):
    position = lax.axis_index("pool")
    number = anchors.shape[0]
    by_token = jnp.transpose(deltas, (1, 0, 2))
    place = jnp.stack([position >> 1, position & 1]).astype(I32)
    lines = jnp.transpose(scales)
    keep, give = decode_halves(place, page_owner, anchors, by_token, lines)
    got = lax.ppermute(give, "pool", TWIN)
    plan = make_plan(place, lengths, page_owner)
    own = (keep, got)
    landed = []
    after = plan
    for time in range(ROUNDS):
        parts = pick(time, plan, place, own, landed, after)
        landed += ship(time, parts)
        after = parts[0]
    partial = attend(plan, queries, anchors, by_token, lines, after)
    swapped = lax.all_to_all(partial, "pool", split_axis=0, concat_axis=0, tiled=True)
    attention = merge(plan, place, swapped)
    cache = finish(plan, place, own, landed, partial)

    def in_time(cache):
        return cache

    def late(cache):
        more, last = list(landed), plan
        for time in range(ROUNDS, LIMIT):
            parts = pick(time, plan, place, own, more, last)
            more += ship(time, parts)
            last = parts[0]
        return finish(plan, place, own, more, last)

    def padded(cache):
        owners = lax.dynamic_slice_in_dim(page_owner, position * number, number, 0)
        index = jnp.arange(number, dtype=I32)
        ahead = (owners[None, :] < owners[:, None]) | (
            (owners[None, :] == owners[:, None]) & (index[None, :] < index[:, None])
        )
        order = jnp.sum(ahead.astype(I32), axis=1)
        devices = jnp.arange(16, dtype=I32)
        sent = jnp.any(owners[None, :] == devices[:, None], axis=1).astype(I32)
        slabs = decode_sorted(order, sent, jnp.cumsum(sent) - sent, anchors, by_token, scales)
        arrived = lax.all_to_all(slabs, "pool", split_axis=0, concat_axis=0, tiled=True)
        taken = jnp.any((page_owner == position).reshape(16, number), axis=1).astype(I32)
        return assemble(taken, jnp.cumsum(taken) - taken, arrived, number)

    needed = plan[2, 0]
    branch = (needed > ROUNDS).astype(I32) + (needed > LIMIT).astype(I32)
    branch, attention = lax.optimization_barrier((branch, attention))
    cache = lax.switch(branch, (in_time, late, padded), cache)
    return (cache, attention)


def decode_pages(anchors, deltas, scales):
    block_scale = jnp.repeat(scales, HD, axis=1)
    rebuilt = anchors[:, None, :].astype(jnp.float32) + block_scale[:, None, :] * deltas.astype(
        jnp.float32
    )
    return jnp.concatenate([anchors[:, None, :], rebuilt.astype(jnp.bfloat16)], axis=1)


def page_scores(work_pages, queries, requests):
    number = work_pages.shape[0]
    key_rows = work_pages[:, :, : KVH * HD].reshape(number, PAGE, KVH, HD)
    picked = jnp.take(queries, requests, axis=0).reshape(number, STEPS, KVH, QH // KVH, HD)
    scores = jnp.einsum(
        "nskgd,ntkd->nskgt", picked, key_rows, preferred_element_type=jnp.float32
    ) * HD ** (-0.5)
    return (scores, jnp.max(scores, axis=4))


def accumulate(scores, page_max, work_pages, requests, shift_max):
    number = work_pages.shape[0]
    rows_out = shift_max.shape[0]
    block_size = min(32, number)
    blocks = number // block_size
    value_rows = work_pages[:, :, KVH * HD :].reshape(blocks, block_size, PAGE, KVH, HD)
    score_blocks = scores.reshape((blocks, block_size) + scores.shape[1:])
    max_blocks = page_max.reshape((blocks, block_size) + page_max.shape[1:])
    request_blocks = requests.reshape(blocks, block_size)

    def block_step(running, pieces):
        totals, numerator = running
        block_scores, block_max, block_values, block_requests = pieces
        exponent = jnp.exp(block_scores - block_max[..., None])
        weights = exponent.astype(jnp.bfloat16)
        page_out = jnp.einsum(
            "nskgt,ntkd->nskgd", weights, block_values, preferred_element_type=jnp.float32
        )
        factor = jnp.exp(block_max - jnp.take(shift_max, block_requests, axis=0))
        select = (block_requests[None, :] == jnp.arange(rows_out, dtype=jnp.int32)[:, None]).astype(
            jnp.float32
        )
        spread = select[:, :, None, None, None] * factor[None]
        totals = totals + jnp.sum(spread * jnp.sum(exponent, axis=4)[None], axis=1)
        numerator = numerator + jnp.einsum(
            "rnskg,nskgd->rskgd", spread, page_out, precision=lax.Precision.HIGHEST
        )
        return ((totals, numerator), None)

    start_totals = jnp.zeros(shift_max.shape, jnp.float32)
    start_numer = jnp.zeros(shift_max.shape + (HD,), jnp.float32)
    finals, ignored = lax.scan(
        block_step,
        (start_totals, start_numer),
        (score_blocks, max_blocks, value_rows, request_blocks),
    )
    return finals


def request_of(index, request_ends):
    return jnp.sum((index[:, None] >= request_ends[None, :]).astype(jnp.int32), axis=1)


def local(anchors, deltas, scales, queries, lengths, page_owner):
    devices = lax.axis_size("pool")
    position = lax.axis_index("pool")
    number = anchors.shape[0]
    capacity = max(2, 2 * number // devices)
    pages = decode_pages(anchors, deltas, scales)
    request_ends = jnp.cumsum(lengths)
    owners = lax.dynamic_slice_in_dim(page_owner, position * number, number, 0)
    marked = (owners[:, None] == jnp.arange(devices, dtype=jnp.int32)[None, :]).astype(jnp.int32)
    ranking = jnp.sum((jnp.cumsum(marked, axis=0) - 1) * marked, axis=1)
    slot_ids = owners * capacity + ranking
    matches = slot_ids[None, :] == jnp.arange(devices * capacity, dtype=jnp.int32)[:, None]
    sources = jnp.sum(jnp.where(matches, jnp.arange(number, dtype=jnp.int32)[None, :], 0), axis=1)
    outgoing = jnp.take(pages, sources, axis=0)
    arrived = lax.all_to_all(outgoing, "pool", split_axis=0, concat_axis=0, tiled=True)
    held_pages = jnp.nonzero(page_owner == position, size=number)[0].astype(jnp.int32)
    senders = held_pages // number
    before = jnp.sum((held_pages[None, :] < (senders * number)[:, None]).astype(jnp.int32), axis=1)
    row_ids = senders * capacity + jnp.arange(number, dtype=jnp.int32) - before
    cache = jnp.take(arrived, row_ids, axis=0)
    columns = QH * HD // devices
    requests = request_of(held_pages, request_ends)
    scores, page_max = page_scores(cache, queries, requests)
    onehot = requests[None, :] == jnp.arange(REQS, dtype=jnp.int32)[:, None]
    local_max = jnp.max(jnp.where(onehot[:, :, None, None, None], page_max[None], -1e30), axis=1)
    global_max = lax.pmax(local_max.astype(jnp.bfloat16), "pool").astype(local_max.dtype)
    totals, numerator = accumulate(scores, page_max, cache, requests, global_max)
    summed, numerator = lax.psum((totals, numerator), "pool")
    whole = (numerator / summed[..., None]).reshape(REQS, STEPS, QH * HD)
    result = lax.dynamic_slice_in_dim(whole, position * columns, columns, 2)
    return (cache, result.astype(jnp.bfloat16))


def solution(mesh):
    placed = (
        P(("groups", "pool"), None),
        P(("groups", "pool"), None, None),
        P(("groups", "pool"), None),
        P("groups", None, None),
        P("groups"),
        P("groups"),
    )
    lanes = mesh.shape["pool"] == 16
    return jax.shard_map(
        local_lanes if lanes else local,
        mesh=mesh,
        in_specs=placed,
        out_specs=(P(("groups", "pool"), None, None), P("groups", None, "pool")),
        check_vma=False,
    )
```

profile of v0, /device:TPU:11, one launch (start us, length us, event | category | flops | bytes accessed | tf_op | source)
XLA Modules:
  0.0 171.4 jit_solution(10454601899337995909)
XLA Ops:
  0.6 0.1 pad_add_fusion.place
  0.7 7.7 %decode_halves.1 = (bf16[64,16,1024]{2,1,0:T(8,128)(2,1)}, bf16[64,16,1024]{2,1,0:T(8,128)(2,1)S(1)}) custom-call(s32[2]{0:T(128)S(1)} %pad_add_fusion.place, s32[16,128]{1,0:T(8,128)} %bitcast.16, bf16[128,1024]{1,0:T(8,128)(2,1)} %val_anchor.1, bf16[15,128,1024]{2,1,0:T(8,128)(2,1)} %bitcast.12, f32[8,128]{1,0:T(8,128)} %bitcast.18), custom_call_target="tpu_custom_call" | custom-call | tf_op jit(solution)/shard_map/decode_halves/pallas_call | solution.py:474
  8.4 0.7 collective-permute-start.10
  9.2 5.0 %make_plan.1.plan.refs_2_.requests = s32[8,128]{1,0:T(8,128)S(1)} custom-call(s32[2]{0:T(128)S(1)} %pad_add_fusion.place, s32[16]{0:T(128)} %lengths.1, s32[16,128]{1,0:T(8,128)S(1)} %bitcast.17), custom_call_target="tpu_custom_call" | custom-call | tf_op jit(solution)/shard_map/make_plan/pallas_call | solution.py:400
  14.1 2.1 %pick_0.1 = (bf16[16,16,1024]{2,1,0:T(8,128)(2,1)S(1)}, bf16[16,16,1024]{2,1,0:T(8,128)(2,1)S(1)}, bf16[24,16,1024]{2,1,0:T(8,128)(2,1)S(1)}) custom-call(s32[8,128]{1,0:T(8,128)S(1)} %make_plan.1.plan.refs_2_.requests, s32[2]{0:T(128)S(1)} %pad_add_fusion.place, bf16[64,16,1024]{2,1,0:T(8,128)(2,1)} %get-tuple-element.143.refs_0_, ...), custom_call_target="tpu_custom_call" | custom-call | tf_op jit(solution)/shard_map/pick_0/pallas_call | solution.py:559
  16.3 0.3 collective-permute-start.13
  16.6 3.2 %collective-permute-start.11 = (bf16[16,16,1024]{2,1,0:T(8,128)(2,1)S(1)}, bf16[16,16,1024]{2,1,0:T(8,128)(2,1)S(1)}, u32[]{:S(2)}, u32[]{:S(2)}) collective-permute-start(bf16[16,16,1024]{2,1,0:T(8,128)(2,1)S(1)} %get-tuple-element.145.refs_2_), channel_id=1, source_target_pairs={{0,4},{1,5},{2,6},{3,7},{4,8},{5,9},{6,10},{7,11},{8,12},{9,13},{1... | collective-permute-start | bytes 1572872 | tf_op jit(solution)/shard_map/ppermute | solution.py:695
  19.8 2.1 %collective-permute-start.12 = (bf16[16,16,1024]{2,1,0:T(8,128)(2,1)S(1)}, bf16[16,16,1024]{2,1,0:T(8,128)(2,1)S(1)}, u32[]{:S(2)}, u32[]{:S(2)}) collective-permute-start(bf16[16,16,1024]{2,1,0:T(8,128)(2,1)S(1)} %get-tuple-element.146), channel_id=1, source_target_pairs={{4,0},{5,1},{6,2},{7,3},{8,4},{9,5},{10,6},{11,7},{12,8},{13,9},{1... | collective-permute-start | bytes 1572872 | tf_op jit(solution)/shard_map/ppermute | solution.py:695
  21.9 1.7 pick_1.1
  23.6 3.2 %collective-permute-start.14 = (bf16[16,16,1024]{2,1,0:T(8,128)(2,1)S(1)}, bf16[16,16,1024]{2,1,0:T(8,128)(2,1)S(1)}, u32[]{:S(2)}, u32[]{:S(2)}) collective-permute-start(bf16[16,16,1024]{2,1,0:T(8,128)(2,1)S(1)} %get-tuple-element.148.refs_4_), channel_id=1, source_target_pairs={{0,4},{1,5},{2,6},{3,7},{4,8},{5,9},{6,10},{7,11},{8,12},{9,13},{1... | collective-permute-start | bytes 1572872 | tf_op jit(solution)/shard_map/ppermute | solution.py:695
  26.8 2.1 %collective-permute-start.15 = (bf16[16,16,1024]{2,1,0:T(8,128)(2,1)S(1)}, bf16[16,16,1024]{2,1,0:T(8,128)(2,1)S(1)}, u32[]{:S(2)}, u32[]{:S(2)}) collective-permute-start(bf16[16,16,1024]{2,1,0:T(8,128)(2,1)S(1)} %get-tuple-element.149), channel_id=1, source_target_pairs={{4,0},{5,1},{6,2},{7,3},{8,4},{9,5},{10,6},{11,7},{12,8},{13,9},{1... | collective-permute-start | bytes 1572872 | tf_op jit(solution)/shard_map/ppermute | solution.py:695
  28.9 2.8 %collective-permute-done.11.refs_2_ = bf16[16,16,1024]{2,1,0:T(8,128)(2,1)S(1)} collective-permute-done((bf16[16,16,1024]{2,1,0:T(8,128)(2,1)S(1)}, bf16[16,16,1024]{2,1,0:T(8,128)(2,1)S(1)}, u32[]{:S(2)}, u32[]{:S(2)}) %collective-permute-start.11) | collective-permute-done | bytes 524320 | tf_op jit(solution)/shard_map/ppermute | solution.py:695
  31.7 2.9 %collective-permute-done.12.refs_3_ = bf16[16,16,1024]{2,1,0:T(8,128)(2,1)S(1)} collective-permute-done((bf16[16,16,1024]{2,1,0:T(8,128)(2,1)S(1)}, bf16[16,16,1024]{2,1,0:T(8,128)(2,1)S(1)}, u32[]{:S(2)}, u32[]{:S(2)}) %collective-permute-start.12) | collective-permute-done | bytes 524320 | tf_op jit(solution)/shard_map/ppermute | solution.py:695
  34.6 0.9 pick_2.1
  35.5 3.9 %collective-permute-start.16 = (bf16[16,16,1024]{2,1,0:T(8,128)(2,1)S(1)}, bf16[16,16,1024]{2,1,0:T(8,128)(2,1)S(1)}, u32[]{:S(2)}, u32[]{:S(2)}) collective-permute-start(bf16[16,16,1024]{2,1,0:T(8,128)(2,1)S(1)} %get-tuple-element.150.refs_7_), channel_id=1, source_target_pairs={{0,4},{1,5},{2,6},{3,7},{4,8},{5,9},{6,10},{7,11},{8,12},{9,13},{1... | collective-permute-start | bytes 1572872 | tf_op jit(solution)/shard_map/ppermute | solution.py:695
  39.4 0.3 collective-permute-start.18
  39.7 3.2 %collective-permute-done.14.refs_5_ = bf16[16,16,1024]{2,1,0:T(8,128)(2,1)S(1)} collective-permute-done((bf16[16,16,1024]{2,1,0:T(8,128)(2,1)S(1)}, bf16[16,16,1024]{2,1,0:T(8,128)(2,1)S(1)}, u32[]{:S(2)}, u32[]{:S(2)}) %collective-permute-start.14) | collective-permute-done | bytes 524320 | tf_op jit(solution)/shard_map/ppermute | solution.py:695
  42.9 1.9 %collective-permute-start.17 = (bf16[16,16,1024]{2,1,0:T(8,128)(2,1)S(1)}, bf16[16,16,1024]{2,1,0:T(8,128)(2,1)S(1)}, u32[]{:S(2)}, u32[]{:S(2)}) collective-permute-start(bf16[16,16,1024]{2,1,0:T(8,128)(2,1)S(1)} %get-tuple-element.151), channel_id=1, source_target_pairs={{4,0},{5,1},{6,2},{7,3},{8,4},{9,5},{10,6},{11,7},{12,8},{13,9},{1... | collective-permute-start | bytes 1572872 | tf_op jit(solution)/shard_map/ppermute | solution.py:695
  44.8 1.0 collective-permute-done.15.refs_6_
  45.8 0.8 pick_3.1
  46.7 3.1 %collective-permute-start.19 = (bf16[16,16,1024]{2,1,0:T(8,128)(2,1)S(1)}, bf16[16,16,1024]{2,1,0:T(8,128)(2,1)S(1)}, u32[]{:S(2)}, u32[]{:S(2)}) collective-permute-start(bf16[16,16,1024]{2,1,0:T(8,128)(2,1)S(1)} %get-tuple-element.153.refs_9_), channel_id=1, source_target_pairs={{0,4},{1,5},{2,6},{3,7},{4,8},{5,9},{6,10},{7,11},{8,12},{9,13},{1... | collective-permute-start | bytes 1572872 | tf_op jit(solution)/shard_map/ppermute | solution.py:695
  49.7 2.3 %collective-permute-start.20 = (bf16[16,16,1024]{2,1,0:T(8,128)(2,1)S(1)}, bf16[16,16,1024]{2,1,0:T(8,128)(2,1)S(1)}, u32[]{:S(2)}, u32[]{:S(2)}) collective-permute-start(bf16[16,16,1024]{2,1,0:T(8,128)(2,1)S(1)} %get-tuple-element.154), channel_id=1, source_target_pairs={{4,0},{5,1},{6,2},{7,3},{8,4},{9,5},{10,6},{11,7},{12,8},{13,9},{1... | collective-permute-start | bytes 1572872 | tf_op jit(solution)/shard_map/ppermute | solution.py:695
  52.0 2.2 %collective-permute-done.16.refs_7_ = bf16[16,16,1024]{2,1,0:T(8,128)(2,1)S(1)} collective-permute-done((bf16[16,16,1024]{2,1,0:T(8,128)(2,1)S(1)}, bf16[16,16,1024]{2,1,0:T(8,128)(2,1)S(1)}, u32[]{:S(2)}, u32[]{:S(2)}) %collective-permute-start.16) | collective-permute-done | bytes 524320 | tf_op jit(solution)/shard_map/ppermute | solution.py:695
  54.1 2.2 %collective-permute-done.17.refs_8_ = bf16[16,16,1024]{2,1,0:T(8,128)(2,1)S(1)} collective-permute-done((bf16[16,16,1024]{2,1,0:T(8,128)(2,1)S(1)}, bf16[16,16,1024]{2,1,0:T(8,128)(2,1)S(1)}, u32[]{:S(2)}, u32[]{:S(2)}) %collective-permute-start.17) | collective-permute-done | bytes 524320 | tf_op jit(solution)/shard_map/ppermute | solution.py:695
  56.4 1.0 pick_4.1
  57.4 1.3 collective-permute-start.23
  58.7 3.2 %collective-permute-start.21 = (bf16[16,16,1024]{2,1,0:T(8,128)(2,1)S(1)}, bf16[16,16,1024]{2,1,0:T(8,128)(2,1)S(1)}, u32[]{:S(2)}, u32[]{:S(2)}) collective-permute-start(bf16[16,16,1024]{2,1,0:T(8,128)(2,1)S(1)} %get-tuple-element.155.refs_12_), channel_id=1, source_target_pairs={{0,4},{1,5},{2,6},{3,7},{4,8},{5,9},{6,10},{7,11},{8,12},{9,13},{1... | collective-permute-start | bytes 1572872 | tf_op jit(solution)/shard_map/ppermute | solution.py:695
  61.9 3.5 %collective-permute-done.19.refs_10_ = bf16[16,16,1024]{2,1,0:T(8,128)(2,1)S(1)} collective-permute-done((bf16[16,16,1024]{2,1,0:T(8,128)(2,1)S(1)}, bf16[16,16,1024]{2,1,0:T(8,128)(2,1)S(1)}, u32[]{:S(2)}, u32[]{:S(2)}) %collective-permute-start.19) | collective-permute-done | bytes 524320 | tf_op jit(solution)/shard_map/ppermute | solution.py:695
  65.4 1.9 %collective-permute-start.22 = (bf16[16,16,1024]{2,1,0:T(8,128)(2,1)S(1)}, bf16[16,16,1024]{2,1,0:T(8,128)(2,1)S(1)}, u32[]{:S(2)}, u32[]{:S(2)}) collective-permute-start(bf16[16,16,1024]{2,1,0:T(8,128)(2,1)S(1)} %get-tuple-element.156), channel_id=1, source_target_pairs={{4,0},{5,1},{6,2},{7,3},{8,4},{9,5},{10,6},{11,7},{12,8},{13,9},{1... | collective-permute-start | bytes 1572872 | tf_op jit(solution)/shard_map/ppermute | solution.py:695
  67.3 0.3 collective-permute-done.20.refs_11_
  67.6 0.9 pick_5.1
  68.5 3.2 %collective-permute-start.24 = (bf16[16,16,1024]{2,1,0:T(8,128)(2,1)S(1)}, bf16[16,16,1024]{2,1,0:T(8,128)(2,1)S(1)}, u32[]{:S(2)}, u32[]{:S(2)}) collective-permute-start(bf16[16,16,1024]{2,1,0:T(8,128)(2,1)S(1)} %get-tuple-element.158.refs_14_), channel_id=1, source_target_pairs={{0,4},{1,5},{2,6},{3,7},{4,8},{5,9},{6,10},{7,11},{8,12},{9,13},{1... | collective-permute-start | bytes 1572872 | tf_op jit(solution)/shard_map/ppermute | solution.py:695
  71.8 2.1 %collective-permute-start.25 = (bf16[16,16,1024]{2,1,0:T(8,128)(2,1)S(1)}, bf16[16,16,1024]{2,1,0:T(8,128)(2,1)S(1)}, u32[]{:S(2)}, u32[]{:S(2)}) collective-permute-start(bf16[16,16,1024]{2,1,0:T(8,128)(2,1)S(1)} %get-tuple-element.159), channel_id=1, source_target_pairs={{4,0},{5,1},{6,2},{7,3},{8,4},{9,5},{10,6},{11,7},{12,8},{13,9},{1... | collective-permute-start | bytes 1572872 | tf_op jit(solution)/shard_map/ppermute | solution.py:695
  73.9 0.3 collective-permute-done.21.refs_12_
  74.2 4.2 %collective-permute-done.22.refs_13_ = bf16[16,16,1024]{2,1,0:T(8,128)(2,1)S(1)} collective-permute-done((bf16[16,16,1024]{2,1,0:T(8,128)(2,1)S(1)}, bf16[16,16,1024]{2,1,0:T(8,128)(2,1)S(1)}, u32[]{:S(2)}, u32[]{:S(2)}) %collective-permute-start.22) | collective-permute-done | bytes 524320 | tf_op jit(solution)/shard_map/ppermute | solution.py:695
  78.4 1.2 pick_6.1
  79.6 4.2 %collective-permute-start.26 = (bf16[16,16,1024]{2,1,0:T(8,128)(2,1)S(1)}, bf16[16,16,1024]{2,1,0:T(8,128)(2,1)S(1)}, u32[]{:S(2)}, u32[]{:S(2)}) collective-permute-start(bf16[16,16,1024]{2,1,0:T(8,128)(2,1)S(1)} %get-tuple-element.160.refs_17_), channel_id=1, source_target_pairs={{0,4},{1,5},{2,6},{3,7},{4,8},{5,9},{6,10},{7,11},{8,12},{9,13},{1... | collective-permute-start | bytes 1572872 | tf_op jit(solution)/shard_map/ppermute | solution.py:695
  83.8 1.9 %collective-permute-start.27 = (bf16[16,16,1024]{2,1,0:T(8,128)(2,1)S(1)}, bf16[16,16,1024]{2,1,0:T(8,128)(2,1)}, u32[]{:S(2)}, u32[]{:S(2)}) collective-permute-start(bf16[16,16,1024]{2,1,0:T(8,128)(2,1)S(1)} %get-tuple-element.161), channel_id=1, source_target_pairs={{4,0},{5,1},{6,2},{7,3},{8,4},{9,5},{10,6},{11,7},{12,8},{13,9},{1... | collective-permute-start | bytes 1572872 | tf_op jit(solution)/shard_map/ppermute | solution.py:695
  85.7 3.9 %collective-permute-done.25.refs_16_ = bf16[16,16,1024]{2,1,0:T(8,128)(2,1)S(1)} collective-permute-done((bf16[16,16,1024]{2,1,0:T(8,128)(2,1)S(1)}, bf16[16,16,1024]{2,1,0:T(8,128)(2,1)S(1)}, u32[]{:S(2)}, u32[]{:S(2)}) %collective-permute-start.25) | collective-permute-done | bytes 524320 | tf_op jit(solution)/shard_map/ppermute | solution.py:695
  89.6 1.3 pick_7.1
  90.9 3.7 %collective-permute-start.29 = (bf16[16,16,1024]{2,1,0:T(8,128)(2,1)S(1)}, bf16[16,16,1024]{2,1,0:T(8,128)(2,1)}, u32[]{:S(2)}, u32[]{:S(2)}) collective-permute-start(bf16[16,16,1024]{2,1,0:T(8,128)(2,1)S(1)} %get-tuple-element.162.refs_19_), channel_id=1, source_target_pairs={{0,4},{1,5},{2,6},{3,7},{4,8},{5,9},{6,10},{7,11},{8,12},{9,13},{1... | collective-permute-start | bytes 1572872 | tf_op jit(solution)/shard_map/ppermute | solution.py:695
  94.6 2.4 %collective-permute-start.30 = (bf16[16,16,1024]{2,1,0:T(8,128)(2,1)S(1)}, bf16[16,16,1024]{2,1,0:T(8,128)(2,1)}, u32[]{:S(2)}, u32[]{:S(2)}) collective-permute-start(bf16[16,16,1024]{2,1,0:T(8,128)(2,1)S(1)} %get-tuple-element.166), channel_id=1, source_target_pairs={{4,0},{5,1},{6,2},{7,3},{8,4},{9,5},{10,6},{11,7},{12,8},{13,9},{1... | collective-permute-start | bytes 1572872 | tf_op jit(solution)/shard_map/ppermute | solution.py:695
  97.1 2.1 %collective-permute-start.28 = (bf16[24,16,1024]{2,1,0:T(8,128)(2,1)S(1)}, bf16[24,16,1024]{2,1,0:T(8,128)(2,1)}, u32[]{:S(2)}, u32[]{:S(2)}) collective-permute-start(bf16[24,16,1024]{2,1,0:T(8,128)(2,1)S(1)} %get-tuple-element.165), channel_id=1, source_target_pairs={{0,2},{1,3},{2,0},{3,1},{4,6},{5,7},{6,4},{7,5},{8,10},{9,11},{10,... | collective-permute-start | bytes 2359304 | tf_op jit(solution)/shard_map/ppermute | solution.py:695
  99.2 0.8 copy-done.32
  100.0 0.0 collective-permute-start.31
  100.0 0.9 collective-permute-done.27.refs_18_
  101.0 1.7 %pick_8.1 = (bf16[16,16,1024]{2,1,0:T(8,128)(2,1)S(1)}, bf16[16,16,1024]{2,1,0:T(8,128)(2,1)S(1)}, bf16[16,16,1024]{2,1,0:T(8,128)(2,1)S(1)}) custom-call(s32[8,128]{1,0:T(8,128)S(1)} %make_plan.1.plan.refs_2_.requests, s32[2]{0:T(128)S(1)} %pad_add_fusion.place, bf16[64,16,1024]{2,1,0:T(8,128)(2,1)S(1)} %copy-done.1, ...), custom_call_target="tpu_custom_call" | custom-call | tf_op jit(solution)/shard_map/pick_8/pallas_call | solution.py:559
  102.7 3.8 %collective-permute-start.32 = (bf16[16,16,1024]{2,1,0:T(8,128)(2,1)S(1)}, bf16[16,16,1024]{2,1,0:T(8,128)(2,1)S(1)}, u32[]{:S(2)}, u32[]{:S(2)}) collective-permute-start(bf16[16,16,1024]{2,1,0:T(8,128)(2,1)S(1)} %get-tuple-element.163.after), channel_id=1, source_target_pairs={{0,4},{1,5},{2,6},{3,7},{4,8},{5,9},{6,10},{7,11},{8,12},{9,13},{1... | collective-permute-start | bytes 1572872 | tf_op jit(solution)/shard_map/ppermute | solution.py:695
  106.5 1.5 collective-permute-done.29.refs_20_
  108.0 1.9 %collective-permute-start.33 = (bf16[16,16,1024]{2,1,0:T(8,128)(2,1)S(1)}, bf16[16,16,1024]{2,1,0:T(8,128)(2,1)S(1)}, u32[]{:S(2)}, u32[]{:S(2)}) collective-permute-start(bf16[16,16,1024]{2,1,0:T(8,128)(2,1)S(1)} %get-tuple-element.168), channel_id=1, source_target_pairs={{4,0},{5,1},{6,2},{7,3},{8,4},{9,5},{10,6},{11,7},{12,8},{13,9},{1... | collective-permute-start | bytes 1572872 | tf_op jit(solution)/shard_map/ppermute | solution.py:695
  109.9 2.3 %collective-permute-done.30.refs_21_ = bf16[16,16,1024]{2,1,0:T(8,128)(2,1)} collective-permute-done((bf16[16,16,1024]{2,1,0:T(8,128)(2,1)S(1)}, bf16[16,16,1024]{2,1,0:T(8,128)(2,1)}, u32[]{:S(2)}, u32[]{:S(2)}) %collective-permute-start.30) | collective-permute-done | bytes 524320 | tf_op jit(solution)/shard_map/ppermute | solution.py:695
  112.2 1.6 collective-permute-start.34
  113.9 10.7 %attend.1.refs_26_ = bf16[16,112,128]{2,1,0:T(8,128)(2,1)} custom-call(s32[8,128]{1,0:T(8,128)S(1)} %make_plan.1.plan.refs_2_.requests, s32[8,128]{1,0:T(8,128)S(1)} %make_plan.1.plan.refs_2_.requests, bf16[16,8,8192]{2,1,0:T(8,128)(2,1)S(1)} %copy-done, bf16[16,8,8192]{2,1,0:T(8,128)(2,1)S(1)} %copy-done, bf16[16,8,8192]{2,1,0:T(8,128)(2,1)S(1)} %copy-done, ...), custom_call_target="tpu_custom_call" | custom-call | tf_op jit(solution)/shard_map/attend/pallas_call | solution.py:138
  124.6 14.5 %collective-permute-done.34.refs_25_ = bf16[16,16,1024]{2,1,0:T(8,128)(2,1)S(1)} collective-permute-done((bf16[16,16,1024]{2,1,0:T(8,128)(2,1)S(1)}, bf16[16,16,1024]{2,1,0:T(8,128)(2,1)S(1)}, u32[]{:S(2)}, u32[]{:S(2)}) %collective-permute-start.34) | collective-permute-done | bytes 524320 | tf_op jit(solution)/shard_map/ppermute | solution.py:695
  139.0 0.8 copy-done.37
  140.0 2.8 %gather_give.3 = bf16[64,16,1024]{2,1,0:T(8,128)(2,1)S(1)} custom-call(s32[8,128]{1,0:T(8,128)S(1)} %make_plan.1.plan.refs_2_.requests, s32[2]{0:T(128)S(1)} %pad_add_fusion.place, bf16[64,16,1024]{2,1,0:T(8,128)(2,1)S(1)} %copy-done.1, bf16[64,16,1024]{2,1,0:T(8,128)(2,1)} %collective-permute-done.10.refs_1_, ...), custom_call_target="tpu_custom_call" | custom-call | tf_op jit(solution)/shard_map/gather_give/pallas_call | solution.py:589
  142.7 6.9 %collective-permute-start.35 = (bf16[64,16,1024]{2,1,0:T(8,128)(2,1)S(1)}, bf16[64,16,1024]{2,1,0:T(8,128)(2,1)}, u32[]{:S(2)}, u32[]{:S(2)}) collective-permute-start(bf16[64,16,1024]{2,1,0:T(8,128)(2,1)S(1)} %gather_give.3), channel_id=1, source_target_pairs={{0,1},{1,0},{2,3},{3,2},{4,5},{5,4},{6,7},{7,6},{8,9},{9,8},{10,11... | collective-permute-start | bytes 6291464 | tf_op jit(solution)/shard_map/ppermute | solution.py:699
  149.6 4.4 %all-to-all-start.1 = ((bf16[16,112,128]{2,1,0:T(8,128)(2,1)}), bf16[16,112,128]{2,1,0:T(8,128)(2,1)S(1)}, u32[]{:S(2)}, u32[]{:S(2)}) async-start(bf16[16,112,128]{2,1,0:T(8,128)(2,1)} %attend.1.refs_26_), calls=%async_computation.1 | async-start | bytes 917504 | tf_op jit(solution)/shard_map/all_to_all | solution.py:720
  154.0 0.5 slice.3
  155.8 3.1 %gather_own.3.cache = bf16[128,16,1024]{2,1,0:T(8,128)(2,1)} custom-call(s32[8,128]{1,0:T(8,128)S(1)} %make_plan.1.plan.refs_2_.requests, s32[2]{0:T(128)S(1)} %pad_add_fusion.place, bf16[64,16,1024]{2,1,0:T(8,128)(2,1)} %get-tuple-element.143.refs_0_, bf16[64,16,1024]{2,1,0:T(8,128)(2,1)} %collective-permute-done.10.refs_1_, ...), custom_call_target="tpu_custom_call" | custom-call | tf_op jit(solution)/shard_map/gather_own/pallas_call | solution.py:626
  158.9 7.2 %all-to-all-done.1.parts = bf16[16,112,128]{2,1,0:T(8,128)(2,1)S(1)} async-done(((bf16[16,112,128]{2,1,0:T(8,128)(2,1)}), bf16[16,112,128]{2,1,0:T(8,128)(2,1)S(1)}, u32[]{:S(2)}, u32[]{:S(2)}) %all-to-all-start.1) | async-done | bytes 458784 | tf_op jit(solution)/shard_map/all_to_all | solution.py:720
  166.1 1.8 %merge.1 = bf16[16,8,512]{2,1,0:T(8,128)(2,1)} custom-call(s32[8,128]{1,0:T(8,128)S(1)} %make_plan.1.plan.refs_2_.requests, s32[2]{0:T(128)S(1)} %pad_add_fusion.place, bf16[16,112,128]{2,1,0:T(8,128)(2,1)S(1)} %all-to-all-done.1.parts), custom_call_target="tpu_custom_call" | custom-call | tf_op jit(solution)/shard_map/merge/pallas_call | solution.py:203
  168.0 2.9 %fill.3 = bf16[128,16,1024]{2,1,0:T(8,128)(2,1)} custom-call(s32[2]{0:T(128)S(1)} %pad_add_fusion.place, bf16[128,16,1024]{2,1,0:T(8,128)(2,1)} %gather_own.3.cache, bf16[64,16,1024]{2,1,0:T(8,128)(2,1)} %collective-permute-done.35.other), custom_call_target="tpu_custom_call", output_to_operand_aliasing={{}: (1, {})} | custom-call | tf_op jit(solution)/shard_map/fill/pallas_call | solution.py:666
  170.9 0.3 conditional.1
  (55 shorter events, 0.1 us)
Async XLA Ops:
  0.6 8.5 %copy-start.38 = (s32[2048]{0:T(1024)S(1)}, s32[2048]{0:T(1024)}, u32[]{:S(2)}) copy-start(s32[2048]{0:T(1024)} %param.14) | copy-start | bytes 24580
  8.4 5.7 %collective-permute-start.10 = (bf16[64,16,1024]{2,1,0:T(8,128)(2,1)S(1)}, bf16[64,16,1024]{2,1,0:T(8,128)(2,1)}, u32[]{:S(2)}, u32[]{:S(2)}) collective-permute-start(bf16[64,16,1024]{2,1,0:T(8,128)(2,1)S(1)} %get-tuple-element.144), channel_id=1, source_target_pairs={{0,1},{1,0},{2,3},{3,2},{4,5},{5,4},{6,7},{7,6},{8,9},{9,8},{10,11... | collective-permute-start | bytes 6291464 | tf_op jit(solution)/shard_map/ppermute | solution.py:710
  14.1 7.8 %copy-start.1 = (bf16[64,16,1024]{2,1,0:T(8,128)(2,1)S(1)}, bf16[64,16,1024]{2,1,0:T(8,128)(2,1)}, u32[]{:S(2)}) copy-start(bf16[64,16,1024]{2,1,0:T(8,128)(2,1)} %get-tuple-element.143.refs_0_) | copy-start | bytes 6291460
  16.3 29.5 %collective-permute-start.13 = (bf16[24,16,1024]{2,1,0:T(8,128)(2,1)S(1)}, bf16[24,16,1024]{2,1,0:T(8,128)(2,1)S(1)}, u32[]{:S(2)}, u32[]{:S(2)}) collective-permute-start(bf16[24,16,1024]{2,1,0:T(8,128)(2,1)S(1)} %get-tuple-element.147), channel_id=1, source_target_pairs={{0,2},{1,3},{2,0},{3,1},{4,6},{5,7},{6,4},{7,5},{8,10},{9,11},{10,... | collective-permute-start | bytes 2359304 | tf_op jit(solution)/shard_map/ppermute | solution.py:695
  16.6 15.1 %collective-permute-start.11 = (bf16[16,16,1024]{2,1,0:T(8,128)(2,1)S(1)}, bf16[16,16,1024]{2,1,0:T(8,128)(2,1)S(1)}, u32[]{:S(2)}, u32[]{:S(2)}) collective-permute-start(bf16[16,16,1024]{2,1,0:T(8,128)(2,1)S(1)} %get-tuple-element.145.refs_2_), channel_id=1, source_target_pairs={{0,4},{1,5},{2,6},{3,7},{4,8},{5,9},{6,10},{7,11},{8,12},{9,13},{1... | collective-permute-start | bytes 1572872 | tf_op jit(solution)/shard_map/ppermute | solution.py:695
  19.8 14.8 %collective-permute-start.12 = (bf16[16,16,1024]{2,1,0:T(8,128)(2,1)S(1)}, bf16[16,16,1024]{2,1,0:T(8,128)(2,1)S(1)}, u32[]{:S(2)}, u32[]{:S(2)}) collective-permute-start(bf16[16,16,1024]{2,1,0:T(8,128)(2,1)S(1)} %get-tuple-element.146), channel_id=1, source_target_pairs={{4,0},{5,1},{6,2},{7,3},{8,4},{9,5},{10,6},{11,7},{12,8},{13,9},{1... | collective-permute-start | bytes 1572872 | tf_op jit(solution)/shard_map/ppermute | solution.py:695
  23.6 19.3 %collective-permute-start.14 = (bf16[16,16,1024]{2,1,0:T(8,128)(2,1)S(1)}, bf16[16,16,1024]{2,1,0:T(8,128)(2,1)S(1)}, u32[]{:S(2)}, u32[]{:S(2)}) collective-permute-start(bf16[16,16,1024]{2,1,0:T(8,128)(2,1)S(1)} %get-tuple-element.148.refs_4_), channel_id=1, source_target_pairs={{0,4},{1,5},{2,6},{3,7},{4,8},{5,9},{6,10},{7,11},{8,12},{9,13},{1... | collective-permute-start | bytes 1572872 | tf_op jit(solution)/shard_map/ppermute | solution.py:695
  26.8 19.0 %collective-permute-start.15 = (bf16[16,16,1024]{2,1,0:T(8,128)(2,1)S(1)}, bf16[16,16,1024]{2,1,0:T(8,128)(2,1)S(1)}, u32[]{:S(2)}, u32[]{:S(2)}) collective-permute-start(bf16[16,16,1024]{2,1,0:T(8,128)(2,1)S(1)} %get-tuple-element.149), channel_id=1, source_target_pairs={{4,0},{5,1},{6,2},{7,3},{8,4},{9,5},{10,6},{11,7},{12,8},{13,9},{1... | collective-permute-start | bytes 1572872 | tf_op jit(solution)/shard_map/ppermute | solution.py:695
  31.7 108.2 %copy-start.3 = (bf16[16,16,1024]{2,1,0:T(8,128)(2,1)}, bf16[16,16,1024]{2,1,0:T(8,128)(2,1)S(1)}, u32[]{:S(2)}) copy-start(bf16[16,16,1024]{2,1,0:T(8,128)(2,1)S(1)} %collective-permute-done.11.refs_2_) | copy-start | bytes 1572868
  34.6 105.3 %copy-start.5 = (bf16[16,16,1024]{2,1,0:T(8,128)(2,1)}, bf16[16,16,1024]{2,1,0:T(8,128)(2,1)S(1)}, u32[]{:S(2)}) copy-start(bf16[16,16,1024]{2,1,0:T(8,128)(2,1)S(1)} %collective-permute-done.12.refs_3_) | copy-start | bytes 1572868
  35.5 18.6 %collective-permute-start.16 = (bf16[16,16,1024]{2,1,0:T(8,128)(2,1)S(1)}, bf16[16,16,1024]{2,1,0:T(8,128)(2,1)S(1)}, u32[]{:S(2)}, u32[]{:S(2)}) collective-permute-start(bf16[16,16,1024]{2,1,0:T(8,128)(2,1)S(1)} %get-tuple-element.150.refs_7_), channel_id=1, source_target_pairs={{0,4},{1,5},{2,6},{3,7},{4,8},{5,9},{6,10},{7,11},{8,12},{9,13},{1... | collective-permute-start | bytes 1572872 | tf_op jit(solution)/shard_map/ppermute | solution.py:695
  39.4 28.2 %collective-permute-start.18 = (bf16[24,16,1024]{2,1,0:T(8,128)(2,1)S(1)}, bf16[24,16,1024]{2,1,0:T(8,128)(2,1)S(1)}, u32[]{:S(2)}, u32[]{:S(2)}) collective-permute-start(bf16[24,16,1024]{2,1,0:T(8,128)(2,1)S(1)} %get-tuple-element.152), channel_id=1, source_target_pairs={{0,2},{1,3},{2,0},{3,1},{4,6},{5,7},{6,4},{7,5},{8,10},{9,11},{10,... | collective-permute-start | bytes 2359304 | tf_op jit(solution)/shard_map/ppermute | solution.py:695
  42.9 97.0 %copy-start.9 = (bf16[16,16,1024]{2,1,0:T(8,128)(2,1)}, bf16[16,16,1024]{2,1,0:T(8,128)(2,1)S(1)}, u32[]{:S(2)}) copy-start(bf16[16,16,1024]{2,1,0:T(8,128)(2,1)S(1)} %collective-permute-done.14.refs_5_) | copy-start | bytes 1572868
  42.9 13.4 %collective-permute-start.17 = (bf16[16,16,1024]{2,1,0:T(8,128)(2,1)S(1)}, bf16[16,16,1024]{2,1,0:T(8,128)(2,1)S(1)}, u32[]{:S(2)}, u32[]{:S(2)}) collective-permute-start(bf16[16,16,1024]{2,1,0:T(8,128)(2,1)S(1)} %get-tuple-element.151), channel_id=1, source_target_pairs={{4,0},{5,1},{6,2},{7,3},{8,4},{9,5},{10,6},{11,7},{12,8},{13,9},{1... | collective-permute-start | bytes 1572872 | tf_op jit(solution)/shard_map/ppermute | solution.py:695
  45.8 94.1 %copy-start.11 = (bf16[16,16,1024]{2,1,0:T(8,128)(2,1)}, bf16[16,16,1024]{2,1,0:T(8,128)(2,1)S(1)}, u32[]{:S(2)}) copy-start(bf16[16,16,1024]{2,1,0:T(8,128)(2,1)S(1)} %collective-permute-done.15.refs_6_) | copy-start | bytes 1572868
  46.7 18.7 %collective-permute-start.19 = (bf16[16,16,1024]{2,1,0:T(8,128)(2,1)S(1)}, bf16[16,16,1024]{2,1,0:T(8,128)(2,1)S(1)}, u32[]{:S(2)}, u32[]{:S(2)}) collective-permute-start(bf16[16,16,1024]{2,1,0:T(8,128)(2,1)S(1)} %get-tuple-element.153.refs_9_), channel_id=1, source_target_pairs={{0,4},{1,5},{2,6},{3,7},{4,8},{5,9},{6,10},{7,11},{8,12},{9,13},{1... | collective-permute-start | bytes 1572872 | tf_op jit(solution)/shard_map/ppermute | solution.py:695
  49.7 17.9 %collective-permute-start.20 = (bf16[16,16,1024]{2,1,0:T(8,128)(2,1)S(1)}, bf16[16,16,1024]{2,1,0:T(8,128)(2,1)S(1)}, u32[]{:S(2)}, u32[]{:S(2)}) collective-permute-start(bf16[16,16,1024]{2,1,0:T(8,128)(2,1)S(1)} %get-tuple-element.154), channel_id=1, source_target_pairs={{4,0},{5,1},{6,2},{7,3},{8,4},{9,5},{10,6},{11,7},{12,8},{13,9},{1... | collective-permute-start | bytes 1572872 | tf_op jit(solution)/shard_map/ppermute | solution.py:695
  54.1 85.7 %copy-start.13 = (bf16[16,16,1024]{2,1,0:T(8,128)(2,1)}, bf16[16,16,1024]{2,1,0:T(8,128)(2,1)S(1)}, u32[]{:S(2)}) copy-start(bf16[16,16,1024]{2,1,0:T(8,128)(2,1)S(1)} %collective-permute-done.16.refs_7_) | copy-start | bytes 1572868
  56.4 83.6 %copy-start.15 = (bf16[16,16,1024]{2,1,0:T(8,128)(2,1)}, bf16[16,16,1024]{2,1,0:T(8,128)(2,1)S(1)}, u32[]{:S(2)}) copy-start(bf16[16,16,1024]{2,1,0:T(8,128)(2,1)S(1)} %collective-permute-done.17.refs_8_) | copy-start | bytes 1572868
  57.4 32.2 %collective-permute-start.23 = (bf16[24,16,1024]{2,1,0:T(8,128)(2,1)S(1)}, bf16[24,16,1024]{2,1,0:T(8,128)(2,1)S(1)}, u32[]{:S(2)}, u32[]{:S(2)}) collective-permute-start(bf16[24,16,1024]{2,1,0:T(8,128)(2,1)S(1)} %get-tuple-element.157), channel_id=1, source_target_pairs={{0,2},{1,3},{2,0},{3,1},{4,6},{5,7},{6,4},{7,5},{8,10},{9,11},{10,... | collective-permute-start | bytes 2359304 | tf_op jit(solution)/shard_map/ppermute | solution.py:695
  58.7 15.5 %collective-permute-start.21 = (bf16[16,16,1024]{2,1,0:T(8,128)(2,1)S(1)}, bf16[16,16,1024]{2,1,0:T(8,128)(2,1)S(1)}, u32[]{:S(2)}, u32[]{:S(2)}) collective-permute-start(bf16[16,16,1024]{2,1,0:T(8,128)(2,1)S(1)} %get-tuple-element.155.refs_12_), channel_id=1, source_target_pairs={{0,4},{1,5},{2,6},{3,7},{4,8},{5,9},{6,10},{7,11},{8,12},{9,13},{1... | collective-permute-start | bytes 1572872 | tf_op jit(solution)/shard_map/ppermute | solution.py:695
  65.4 74.5 %copy-start.19 = (bf16[16,16,1024]{2,1,0:T(8,128)(2,1)}, bf16[16,16,1024]{2,1,0:T(8,128)(2,1)S(1)}, u32[]{:S(2)}) copy-start(bf16[16,16,1024]{2,1,0:T(8,128)(2,1)S(1)} %collective-permute-done.19.refs_10_) | copy-start | bytes 1572868
  65.4 13.0 %collective-permute-start.22 = (bf16[16,16,1024]{2,1,0:T(8,128)(2,1)S(1)}, bf16[16,16,1024]{2,1,0:T(8,128)(2,1)S(1)}, u32[]{:S(2)}, u32[]{:S(2)}) collective-permute-start(bf16[16,16,1024]{2,1,0:T(8,128)(2,1)S(1)} %get-tuple-element.156), channel_id=1, source_target_pairs={{4,0},{5,1},{6,2},{7,3},{8,4},{9,5},{10,6},{11,7},{12,8},{13,9},{1... | collective-permute-start | bytes 1572872 | tf_op jit(solution)/shard_map/ppermute | solution.py:695
  67.6 33.4 %copy-start.21 = (bf16[16,16,1024]{2,1,0:T(8,128)(2,1)}, bf16[16,16,1024]{2,1,0:T(8,128)(2,1)S(1)}, u32[]{:S(2)}) copy-start(bf16[16,16,1024]{2,1,0:T(8,128)(2,1)S(1)} %collective-permute-done.20.refs_11_) | copy-start | bytes 1572868
  67.6 72.3 %copy-start.7 = (bf16[24,16,1024]{2,1,0:T(8,128)(2,1)}, bf16[24,16,1024]{2,1,0:T(8,128)(2,1)S(1)}, u32[]{:S(2)}) copy-start(bf16[24,16,1024]{2,1,0:T(8,128)(2,1)S(1)} %collective-permute-done.18.refs_9_) | copy-start | bytes 2359300
  68.5 17.2 %collective-permute-start.24 = (bf16[16,16,1024]{2,1,0:T(8,128)(2,1)S(1)}, bf16[16,16,1024]{2,1,0:T(8,128)(2,1)S(1)}, u32[]{:S(2)}, u32[]{:S(2)}) collective-permute-start(bf16[16,16,1024]{2,1,0:T(8,128)(2,1)S(1)} %get-tuple-element.158.refs_14_), channel_id=1, source_target_pairs={{0,4},{1,5},{2,6},{3,7},{4,8},{5,9},{6,10},{7,11},{8,12},{9,13},{1... | collective-permute-start | bytes 1572872 | tf_op jit(solution)/shard_map/ppermute | solution.py:695
  71.8 17.9 %collective-permute-start.25 = (bf16[16,16,1024]{2,1,0:T(8,128)(2,1)S(1)}, bf16[16,16,1024]{2,1,0:T(8,128)(2,1)S(1)}, u32[]{:S(2)}, u32[]{:S(2)}) collective-permute-start(bf16[16,16,1024]{2,1,0:T(8,128)(2,1)S(1)} %get-tuple-element.159), channel_id=1, source_target_pairs={{4,0},{5,1},{6,2},{7,3},{8,4},{9,5},{10,6},{11,7},{12,8},{13,9},{1... | collective-permute-start | bytes 1572872 | tf_op jit(solution)/shard_map/ppermute | solution.py:695
  74.2 26.8 %copy-start.24 = (bf16[16,16,1024]{2,1,0:T(8,128)(2,1)}, bf16[16,16,1024]{2,1,0:T(8,128)(2,1)S(1)}, u32[]{:S(2)}) copy-start(bf16[16,16,1024]{2,1,0:T(8,128)(2,1)S(1)} %collective-permute-done.21.refs_12_) | copy-start | bytes 1572868
  78.4 22.6 %copy-start.26 = (bf16[16,16,1024]{2,1,0:T(8,128)(2,1)}, bf16[16,16,1024]{2,1,0:T(8,128)(2,1)S(1)}, u32[]{:S(2)}) copy-start(bf16[16,16,1024]{2,1,0:T(8,128)(2,1)S(1)} %collective-permute-done.22.refs_13_) | copy-start | bytes 1572868
  79.6 19.6 %collective-permute-start.26 = (bf16[16,16,1024]{2,1,0:T(8,128)(2,1)S(1)}, bf16[16,16,1024]{2,1,0:T(8,128)(2,1)S(1)}, u32[]{:S(2)}, u32[]{:S(2)}) collective-permute-start(bf16[16,16,1024]{2,1,0:T(8,128)(2,1)S(1)} %get-tuple-element.160.refs_17_), channel_id=1, source_target_pairs={{0,4},{1,5},{2,6},{3,7},{4,8},{5,9},{6,10},{7,11},{8,12},{9,13},{1... | collective-permute-start | bytes 1572872 | tf_op jit(solution)/shard_map/ppermute | solution.py:695
  83.8 17.2 %collective-permute-start.27 = (bf16[16,16,1024]{2,1,0:T(8,128)(2,1)S(1)}, bf16[16,16,1024]{2,1,0:T(8,128)(2,1)}, u32[]{:S(2)}, u32[]{:S(2)}) collective-permute-start(bf16[16,16,1024]{2,1,0:T(8,128)(2,1)S(1)} %get-tuple-element.161), channel_id=1, source_target_pairs={{4,0},{5,1},{6,2},{7,3},{8,4},{9,5},{10,6},{11,7},{12,8},{13,9},{1... | collective-permute-start | bytes 1572872 | tf_op jit(solution)/shard_map/ppermute | solution.py:695
  85.7 15.2 %copy-start.28 = (bf16[16,16,1024]{2,1,0:T(8,128)(2,1)}, bf16[16,16,1024]{2,1,0:T(8,128)(2,1)S(1)}, u32[]{:S(2)}) copy-start(bf16[16,16,1024]{2,1,0:T(8,128)(2,1)S(1)} %collective-permute-done.24.refs_15_) | copy-start | bytes 1572868
  89.6 1.3 copy-start.30
  89.6 50.3 %copy-start.17 = (bf16[24,16,1024]{2,1,0:T(8,128)(2,1)}, bf16[24,16,1024]{2,1,0:T(8,128)(2,1)S(1)}, u32[]{:S(2)}) copy-start(bf16[24,16,1024]{2,1,0:T(8,128)(2,1)S(1)} %collective-permute-done.23.refs_14_) | copy-start | bytes 2359300
  90.9 17.1 %collective-permute-start.29 = (bf16[16,16,1024]{2,1,0:T(8,128)(2,1)S(1)}, bf16[16,16,1024]{2,1,0:T(8,128)(2,1)}, u32[]{:S(2)}, u32[]{:S(2)}) collective-permute-start(bf16[16,16,1024]{2,1,0:T(8,128)(2,1)S(1)} %get-tuple-element.162.refs_19_), channel_id=1, source_target_pairs={{0,4},{1,5},{2,6},{3,7},{4,8},{5,9},{6,10},{7,11},{8,12},{9,13},{1... | collective-permute-start | bytes 1572872 | tf_op jit(solution)/shard_map/ppermute | solution.py:695
  94.6 17.6 %collective-permute-start.30 = (bf16[16,16,1024]{2,1,0:T(8,128)(2,1)S(1)}, bf16[16,16,1024]{2,1,0:T(8,128)(2,1)}, u32[]{:S(2)}, u32[]{:S(2)}) collective-permute-start(bf16[16,16,1024]{2,1,0:T(8,128)(2,1)S(1)} %get-tuple-element.166), channel_id=1, source_target_pairs={{4,0},{5,1},{6,2},{7,3},{8,4},{9,5},{10,6},{11,7},{12,8},{13,9},{1... | collective-permute-start | bytes 1572872 | tf_op jit(solution)/shard_map/ppermute | solution.py:695
  97.1 27.5 %collective-permute-start.28 = (bf16[24,16,1024]{2,1,0:T(8,128)(2,1)S(1)}, bf16[24,16,1024]{2,1,0:T(8,128)(2,1)}, u32[]{:S(2)}, u32[]{:S(2)}) collective-permute-start(bf16[24,16,1024]{2,1,0:T(8,128)(2,1)S(1)} %get-tuple-element.165), channel_id=1, source_target_pairs={{0,2},{1,3},{2,0},{3,1},{4,6},{5,7},{6,4},{7,5},{8,10},{9,11},{10,... | collective-permute-start | bytes 2359304 | tf_op jit(solution)/shard_map/ppermute | solution.py:695
  99.2 0.8 copy-start.32
  100.0 13.9 %copy-start = (bf16[16,8,8192]{2,1,0:T(8,128)(2,1)S(1)}, bf16[16,8,8192]{2,1,0:T(8,128)(2,1)}, u32[]{:S(2)}) copy-start(bf16[16,8,8192]{2,1,0:T(8,128)(2,1)} %third.1) | copy-start | bytes 6291460
  100.0 13.9 %copy-start.39 = (f32[128,8]{0,1:T(8,128)S(1)}, f32[128,8]{0,1:T(8,128)}, u32[]{:S(2)}) copy-start(f32[128,8]{0,1:T(8,128)} %param.11) | copy-start | bytes 12292
  100.0 39.9 %collective-permute-start.31 = (bf16[24,16,1024]{2,1,0:T(8,128)(2,1)S(1)}, bf16[24,16,1024]{2,1,0:T(8,128)(2,1)}, u32[]{:S(2)}, u32[]{:S(2)}) collective-permute-start(bf16[24,16,1024]{2,1,0:T(8,128)(2,1)S(1)} %get-tuple-element.167), channel_id=1, source_target_pairs={{0,2},{1,3},{2,0},{3,1},{4,6},{5,7},{6,4},{7,5},{8,10},{9,11},{10,... | collective-permute-start | bytes 2359304 | tf_op jit(solution)/shard_map/ppermute | solution.py:695
  102.7 21.8 %collective-permute-start.32 = (bf16[16,16,1024]{2,1,0:T(8,128)(2,1)S(1)}, bf16[16,16,1024]{2,1,0:T(8,128)(2,1)S(1)}, u32[]{:S(2)}, u32[]{:S(2)}) collective-permute-start(bf16[16,16,1024]{2,1,0:T(8,128)(2,1)S(1)} %get-tuple-element.163.after), channel_id=1, source_target_pairs={{0,4},{1,5},{2,6},{3,7},{4,8},{5,9},{6,10},{7,11},{8,12},{9,13},{1... | collective-permute-start | bytes 1572872 | tf_op jit(solution)/shard_map/ppermute | solution.py:695
  108.0 16.5 %collective-permute-start.33 = (bf16[16,16,1024]{2,1,0:T(8,128)(2,1)S(1)}, bf16[16,16,1024]{2,1,0:T(8,128)(2,1)S(1)}, u32[]{:S(2)}, u32[]{:S(2)}) collective-permute-start(bf16[16,16,1024]{2,1,0:T(8,128)(2,1)S(1)} %get-tuple-element.168), channel_id=1, source_target_pairs={{4,0},{5,1},{6,2},{7,3},{8,4},{9,5},{10,6},{11,7},{12,8},{13,9},{1... | collective-permute-start | bytes 1572872 | tf_op jit(solution)/shard_map/ppermute | solution.py:695
  112.2 27.7 %copy-start.22 = (bf16[16,16,1024]{2,1,0:T(8,128)(2,1)S(1)}, bf16[16,16,1024]{2,1,0:T(8,128)(2,1)}, u32[]{:S(2)}) copy-start(bf16[16,16,1024]{2,1,0:T(8,128)(2,1)} %copy-done.21) | copy-start | bytes 1572868
  112.2 26.8 %collective-permute-start.34 = (bf16[16,16,1024]{2,1,0:T(8,128)(2,1)S(1)}, bf16[16,16,1024]{2,1,0:T(8,128)(2,1)S(1)}, u32[]{:S(2)}, u32[]{:S(2)}) collective-permute-start(bf16[16,16,1024]{2,1,0:T(8,128)(2,1)S(1)} %get-tuple-element.169), channel_id=1, source_target_pairs={{0,2},{1,3},{2,0},{3,1},{4,6},{5,7},{6,4},{7,5},{8,10},{9,11},{10,... | collective-permute-start | bytes 1572872 | tf_op jit(solution)/shard_map/ppermute | solution.py:695
  124.5 14.5 %copy-start.34 = (bf16[16,16,1024]{2,1,0:T(8,128)(2,1)}, bf16[16,16,1024]{2,1,0:T(8,128)(2,1)S(1)}, u32[]{:S(2)}) copy-start(bf16[16,16,1024]{2,1,0:T(8,128)(2,1)S(1)} %collective-permute-done.32.refs_23_) | copy-start | bytes 1572868
  124.6 14.5 %copy-start.36 = (bf16[16,16,1024]{2,1,0:T(8,128)(2,1)}, bf16[16,16,1024]{2,1,0:T(8,128)(2,1)S(1)}, u32[]{:S(2)}) copy-start(bf16[16,16,1024]{2,1,0:T(8,128)(2,1)S(1)} %collective-permute-done.33.refs_24_) | copy-start | bytes 1572868
  139.0 0.8 copy-start.37
  142.7 25.2 %collective-permute-start.35 = (bf16[64,16,1024]{2,1,0:T(8,128)(2,1)S(1)}, bf16[64,16,1024]{2,1,0:T(8,128)(2,1)}, u32[]{:S(2)}, u32[]{:S(2)}) collective-permute-start(bf16[64,16,1024]{2,1,0:T(8,128)(2,1)S(1)} %gather_give.3), channel_id=1, source_target_pairs={{0,1},{1,0},{2,3},{3,2},{4,5},{5,4},{6,7},{7,6},{8,9},{9,8},{10,11... | collective-permute-start | bytes 6291464 | tf_op jit(solution)/shard_map/ppermute | solution.py:699
  149.6 16.5 %all-to-all-start.1 = ((bf16[16,112,128]{2,1,0:T(8,128)(2,1)}), bf16[16,112,128]{2,1,0:T(8,128)(2,1)S(1)}, u32[]{:S(2)}, u32[]{:S(2)}) async-start(bf16[16,112,128]{2,1,0:T(8,128)(2,1)} %attend.1.refs_26_), calls=%async_computation.1 | async-start | bytes 917504 | tf_op jit(solution)/shard_map/all_to_all | solution.py:720
where the time goes:
time: 174 us; the launch traced here: 171 us
  starting transfers between devices  67.8 us (39%)
  waiting for transfers between devices  52.8 us (30%)
  Pallas kernels  45.7 us (26%)
  between operations  2.56 us (1%)
  local copies, waits for them, and re-layouts  2.21 us (1%)
    ppermute x24, starting transfers between devices, ship(): lax.ppermute(part, 'pool', hops[port])  55.8 us
    ppermute x24, waiting for transfers between devices, ship(): lax.ppermute(part, 'pool', hops[port])  45.5 us
    pallas_call x9, Pallas kernels, pick(): pl.pallas_call(functools.partial(pick_kernel, time, [item[:2] for item in...  11.7 us
    pallas_call x1, Pallas kernels, attend(): pl.pallas_call(attend_kernel, grid_spec=pltpu.PrefetchScalarGridSpec(num_...  10.7 us
    pallas_call x1, Pallas kernels, decode_halves(): pl.pallas_call(halves_kernel, grid_spec=pltpu.PrefetchScalarGridSpec(num_...  7.69 us
    all_to_all x1, waiting for transfers between devices, local_lanes(): lax.all_to_all(partial, 'pool', split_axis=0, concat_axis=0, tiled=True)  7.23 us
    ppermute x1, starting transfers between devices, finish(): lax.ppermute(gather_give(plan, place, own, landed, after), 'pool', TWIN)  6.86 us
    pallas_call x1, Pallas kernels, make_plan(): pl.pallas_call(plan_kernel, grid_spec=pltpu.PrefetchScalarGridSpec(num_sc...  4.97 us
  transfers between devices with their start and end apart: 27, of which 16 were waited for; matrix products, arithmetic and copies ran while one was open for 0% of the time, Pallas kernels for 18%

commit v1 on v0

--- a/solution.py
+++ b/solution.py
@@ -79,13 +79,11 @@
     )(place, flags, blocks, anchors, deltas, scales)
 
 
-def attend_kernel(plan, requests, first, second, third, key_anchor, val_anchor, key_delta, val_delta, scales, after, out, keys, vals):
-    head = pl.program_id(0)
+def attend_kernel(head, plan, requests, first, second, third, key_anchor, val_anchor, key_delta, val_delta, scales, after, out, keys, vals):
     number = key_anchor.shape[0]
-    table = jnp.transpose(scales[...])
-    lane = lax.broadcasted_iota(I32, table.shape, 1)
-    key_scale = jnp.sum(jnp.where(lane == head, table, 0.0), axis=1, keepdims=True)
-    val_scale = jnp.sum(jnp.where(lane == head + KVH, table, 0.0), axis=1, keepdims=True)
+    columns = jnp.transpose(scales[...])
+    key_scale = columns[:, head : head + 1]
+    val_scale = columns[:, head + KVH : head + KVH + 1]
     for anchor, delta, scale, kept in (
         (key_anchor, key_delta, key_scale, keys),
         (val_anchor, val_delta, val_scale, vals),
@@ -132,36 +130,37 @@
         out[part, 96:112, :] = stats
 
 
-def attend(plan, queries, anchors, deltas, scales, after):
+def attend(head, plan, queries, anchors, deltas, scales, after):
     number = anchors.shape[0]
     rows = STEPS * QH // KVH
     return pl.pallas_call(
-        attend_kernel,
+        functools.partial(attend_kernel, head),
         grid_spec=pltpu.PrefetchScalarGridSpec(
             num_scalar_prefetch=1,
-            grid=(KVH,),
+            grid=(1,),
             in_specs=[
-                pl.BlockSpec((8, number), lambda h, *_: (0, 0)),
+                pl.BlockSpec((8, number), lambda i, *_: (0, 0)),
                 *[
-                    pl.BlockSpec((1, STEPS, rows * HD // STEPS), lambda h, p, k=k: (p[5, 0] + k, 0, h))
+                    pl.BlockSpec((1, STEPS, rows * HD // STEPS), lambda i, p, k=k: (p[5, 0] + k, 0, head))
                     for k in range(SPAN)
                 ],
-                pl.BlockSpec((number, HD), lambda h, *_: (0, h)),
-                pl.BlockSpec((number, HD), lambda h, *_: (0, h + KVH)),
-                pl.BlockSpec((PAGE - 1, number, HD), lambda h, *_: (0, 0, h)),
-                pl.BlockSpec((PAGE - 1, number, HD), lambda h, *_: (0, 0, h + KVH)),
-                pl.BlockSpec((2 * KVH, number), lambda h, *_: (0, 0)),
+                pl.BlockSpec((number, HD), lambda i, *_: (0, head)),
+                pl.BlockSpec((number, HD), lambda i, *_: (0, head + KVH)),
+                pl.BlockSpec((PAGE - 1, number, HD), lambda i, *_: (0, 0, head)),
+                pl.BlockSpec((PAGE - 1, number, HD), lambda i, *_: (0, 0, head + KVH)),
+                pl.BlockSpec((2 * KVH, number), lambda i, *_: (0, 0)),
                 pl.BlockSpec(memory_space=pl.ANY),
             ],
-            out_specs=pl.BlockSpec((4, 112, HD), lambda h, *_: (h, 0, 0)),
+            out_specs=pl.BlockSpec((4, 112, HD), lambda i, *_: (head, 0, 0)),
             scratch_shapes=[
                 pltpu.VMEM((PAGE * number, HD), BF16),
                 pltpu.VMEM((PAGE * number, HD), BF16),
             ],
         ),
         out_shape=jax.ShapeDtypeStruct((16, 112, HD), BF16),
+        input_output_aliases={} if head == 0 else {10: 0},
         compiler_params=pltpu.CompilerParams(vmem_limit_bytes=VMEM_LIMIT),
-        name="attend",
+        name=f"attend_{head}",
     )(plan, plan, queries, queries, queries, anchors, anchors, deltas, deltas, scales, after)
 
 
@@ -266,6 +265,7 @@
 LAG = 2
 SIDE_LAG = 3
 SLOTS = 7
+SIDE = (3, 0, 3, 0, 3, 0, 2, 2, 1)
 HALF = PAGE // 2
 FAR = 1e6
 
@@ -273,9 +273,7 @@
 def units_of(port, time):
     if port < 2:
         return UNIT
-    if time >= 8:
-        return 2
-    return 3 if time in (0, 2, 4, 6, 7) else 0
+    return SIDE[time] if time < len(SIDE) else 2
 
 
 def plan_kernel(place, lengths, owners, out):
@@ -571,11 +569,15 @@
     )(plan, place, *sources)
 
 
+def known(code, tags):
+    return jnp.where(code > 16 + SLOTS * (1 + max(time for time, _ in tags)), 0, code)
+
+
 def give_kernel(tags, plan, place, *refs):
     own, landed = refs[:2], [tag + (ref,) for tag, ref in zip(tags, refs[2:])]
     out, sems = refs[-2:]
     core = place[1]
-    codes = [plan[1, (1 - core) * 8 + slot] for slot in range(8)]
+    codes = [known(plan[1, (1 - core) * 8 + slot], tags) for slot in range(8)]
     targets = [out.at[pl.ds(slot * HALF, HALF)] for slot in range(8)]
     for slot in range(8):
         fetch(codes[slot], core, own, landed, (0, 1, 2), targets[slot], sems.at[slot])
@@ -605,7 +607,7 @@
     own, landed = refs[:2], [tag + (ref,) for tag, ref in zip(tags, refs[2:])]
     out, staged, in_sems, out_sems = refs[-4:]
     core = place[1]
-    codes = [plan[1, core * 8 + slot] for slot in range(8)]
+    codes = [known(plan[1, core * 8 + slot], tags) for slot in range(8)]
     targets = [staged.at[pl.ds(slot * HALF, HALF)] for slot in range(8)]
     for slot in range(8):
         fetch(codes[slot], core, own, landed, (0, 1, 2), targets[slot], in_sems.at[slot])
@@ -711,15 +713,18 @@
     plan = make_plan(place, lengths, page_owner)
     own = (keep, got)
     landed = []
-    after = plan
+    after = partial = plan
     for time in range(ROUNDS):
         parts = pick(time, plan, place, own, landed, after)
         landed += ship(time, parts)
         after = parts[0]
-    partial = attend(plan, queries, anchors, by_token, lines, after)
+        if 1 <= time <= KVH:
+            seen, _ = lax.optimization_barrier((plan, after))
+            after = partial = attend(time - 1, seen, queries, anchors, by_token, lines, partial)
+    partial, _ = lax.optimization_barrier((partial, after))
     swapped = lax.all_to_all(partial, "pool", split_axis=0, concat_axis=0, tiled=True)
     attention = merge(plan, place, swapped)
-    cache = finish(plan, place, own, landed, partial)
+    cache = finish(plan, place, own, landed, attention)
 
     def in_time(cache):
         return cache

time: 174 us -> 236 us (1.36)
  Pallas kernels: 45.7 us -> 75.5 us
  starting transfers between devices: 67.8 us -> 82.4 us
  waiting for transfers between devices: 52.8 us -> 65.4 us
    ppermute x24 -> x33, waiting for transfers between devices: 45.5 us -> 65.2 us  [ship(): lax.ppermute(part, 'pool', hops[port])]
    pallas_call x9 -> x12, Pallas kernels: 11.7 us -> 27.9 us  [pick(): pl.pallas_call(functools.partial(pick_kernel, time, [item[:2] for item in...]
    ppermute x24 -> x33, starting transfers between devices: 55.8 us -> 70.5 us  [ship(): lax.ppermute(part, 'pool', hops[port])]
    all_to_all x1, waiting for transfers between devices: 7.23 us -> 0.01 us  [local_lanes(): lax.all_to_all(partial, 'pool', split_axis=0, concat_axis=0, tiled=True)]
    pallas_call x1 -> x2, Pallas kernels: 3.12 us -> 7.47 us  [gather_own(): pl.pallas_call(functools.partial(own_kernel, [item[:2] for item in landed...]
    pallas_call x1 -> x2, Pallas kernels: 2.78 us -> 7.11 us  [gather_give(): pl.pallas_call(functools.partial(give_kernel, [item[:2] for item in lande...]
    ppermute x1 -> x2, starting transfers between devices: 6.86 us -> 3.05 us  [finish(): lax.ppermute(gather_give(plan, place, own, landed, after), 'pool', TWIN)]
    all_to_all x1, starting transfers between devices: 4.37 us -> 8.15 us  [local_lanes(): lax.all_to_all(partial, 'pool', split_axis=0, concat_axis=0, tiled=True)]
  transfers between devices with their start and end apart: 27 -> 37, of which waited for: 16 -> 17; matrix products, arithmetic and copies ran while one was open for 0% -> 0% of each run, Pallas kernels for 18% -> 22%
where the time goes in v1:
time: 236 us; the launch traced here: 232 us
  starting transfers between devices  82.4 us (35%)
  Pallas kernels  75.5 us (32%)
  waiting for transfers between devices  65.4 us (28%)
  local copies, waits for them, and re-layouts  3.99 us (2%)
  between operations  3.82 us (2%)
    ppermute x33, starting transfers between devices, ship(): lax.ppermute(part, 'pool', hops[port])  70.5 us
    ppermute x33, waiting for transfers between devices, ship(): lax.ppermute(part, 'pool', hops[port])  65.2 us
    pallas_call x12, Pallas kernels, pick(): pl.pallas_call(functools.partial(pick_kernel, time, [item[:2] for item in...  27.9 us
    pallas_call x4, Pallas kernels, attend(): pl.pallas_call(functools.partial(attend_kernel, head), grid_spec=pltpu.Pr...  13.5 us
    all_to_all x1, starting transfers between devices, local_lanes(): lax.all_to_all(partial, 'pool', split_axis=0, concat_axis=0, tiled=True)  8.15 us
    pallas_call x1, Pallas kernels, decode_halves(): pl.pallas_call(halves_kernel, grid_spec=pltpu.PrefetchScalarGridSpec(num_...  7.67 us
    pallas_call x2, Pallas kernels, gather_own(): pl.pallas_call(functools.partial(own_kernel, [item[:2] for item in landed...  7.47 us
    pallas_call x2, Pallas kernels, gather_give(): pl.pallas_call(functools.partial(give_kernel, [item[:2] for item in lande...  7.11 us
  transfers between devices with their start and end apart: 37, of which 17 were waited for; matrix products, arithmetic and copies ran while one was open for 0% of the time, Pallas kernels for 22%

profile of v1, /device:TPU:11, one launch (start us, length us, event | category | flops | bytes accessed | tf_op | source)
XLA Modules:
  0.0 232.5 jit_solution(4157232752563775021)
XLA Ops:
  0.7 7.7 %decode_halves.1 = (bf16[64,16,1024]{2,1,0:T(8,128)(2,1)}, bf16[64,16,1024]{2,1,0:T(8,128)(2,1)S(1)}) custom-call(s32[2]{0:T(128)S(1)} %pad_add_fusion.place, s32[16,128]{1,0:T(8,128)} %bitcast.27, bf16[128,1024]{1,0:T(8,128)(2,1)} %val_anchor.7, bf16[15,128,1024]{2,1,0:T(8,128)(2,1)} %bitcast.12, f32[8,128]{1,0:T(8,128)} %bitcast.22), custom_call_target="tpu_custom_call" | custom-call | tf_op jit(solution)/shard_map/decode_halves/pallas_call | solution.py:472
  9.1 5.0 %make_plan.1.plan.refs_2_.requests.after = s32[8,128]{1,0:T(8,128)S(1)} custom-call(s32[2]{0:T(128)S(1)} %pad_add_fusion.place, s32[16]{0:T(128)} %lengths.1, s32[16,128]{1,0:T(8,128)S(1)} %bitcast.28), custom_call_target="tpu_custom_call" | custom-call | tf_op jit(solution)/shard_map/make_plan/pallas_call | solution.py:398
  14.2 2.4 %pick_0.1 = (bf16[16,16,1024]{2,1,0:T(8,128)(2,1)S(1)}, bf16[16,16,1024]{2,1,0:T(8,128)(2,1)S(1)}, bf16[24,16,1024]{2,1,0:T(8,128)(2,1)S(1)}) custom-call(s32[8,128]{1,0:T(8,128)S(1)} %make_plan.1.plan.refs_2_.requests.after, s32[2]{0:T(128)S(1)} %pad_add_fusion.place, bf16[64,16,1024]{2,1,0:T(8,128)(2,1)} %get-tuple-element.148.refs_0_, ...), custom_call_target="tpu_custom_call" | custom-call | tf_op jit(solution)/shard_map/pick_0/pallas_call | solution.py:557
  16.6 3.3 %collective-permute-start.11 = (bf16[16,16,1024]{2,1,0:T(8,128)(2,1)S(1)}, bf16[16,16,1024]{2,1,0:T(8,128)(2,1)S(1)}, u32[]{:S(2)}, u32[]{:S(2)}) collective-permute-start(bf16[16,16,1024]{2,1,0:T(8,128)(2,1)S(1)} %get-tuple-element.150.refs_2_), channel_id=1, source_target_pairs={{0,4},{1,5},{2,6},{3,7},{4,8},{5,9},{6,10},{7,11},{8,12},{9,13},{1... | collective-permute-start | bytes 1572872 | tf_op jit(solution)/shard_map/ppermute | solution.py:697
  19.9 2.1 collective-permute-start.12
  22.4 1.7 pick_1.1
  24.1 3.1 %collective-permute-start.14 = (bf16[16,16,1024]{2,1,0:T(8,128)(2,1)S(1)}, bf16[16,16,1024]{2,1,0:T(8,128)(2,1)S(1)}, u32[]{:S(2)}, u32[]{:S(2)}) collective-permute-start(bf16[16,16,1024]{2,1,0:T(8,128)(2,1)S(1)} %get-tuple-element.153), channel_id=1, source_target_pairs={{0,4},{1,5},{2,6},{3,7},{4,8},{5,9},{6,10},{7,11},{8,12},{9,13},{1... | collective-permute-start | bytes 1572872 | tf_op jit(solution)/shard_map/ppermute | solution.py:697
  27.2 2.2 collective-permute-start.15
  29.5 3.4 %attend_0.1.refs_4_.after = bf16[16,112,128]{2,1,0:T(8,128)(2,1)} custom-call(s32[8,128]{1,0:T(8,128)S(1)} %make_plan.1.plan.refs_2_.requests.after, s32[8,128]{1,0:T(8,128)S(1)} %make_plan.1.plan.refs_2_.requests.after, bf16[16,8,8192]{2,1,0:T(8,128)(2,1)S(1)} %copy-done, bf16[16,8,8192]{2,1,0:T(8,128)(2,1)S(1)} %copy-done, ...), custom_call_target="tpu_custom_call" | custom-call | tf_op jit(solution)/shard_map/attend_0/pallas_call | solution.py:136
  32.8 2.2 collective-permute-done.12.refs_3_
  35.9 3.1 %collective-permute-start.16 = (bf16[16,16,1024]{2,1,0:T(8,128)(2,1)S(1)}, bf16[16,16,1024]{2,1,0:T(8,128)(2,1)}, u32[]{:S(2)}, u32[]{:S(2)}) collective-permute-start(bf16[16,16,1024]{2,1,0:T(8,128)(2,1)S(1)} %get-tuple-element.156), channel_id=1, source_target_pairs={{0,4},{1,5},{2,6},{3,7},{4,8},{5,9},{6,10},{7,11},{8,12},{9,13},{1... | collective-permute-start | bytes 1572872 | tf_op jit(solution)/shard_map/ppermute | solution.py:697
  39.0 3.0 %collective-permute-start.17 = (bf16[16,16,1024]{2,1,0:T(8,128)(2,1)S(1)}, bf16[16,16,1024]{2,1,0:T(8,128)(2,1)}, u32[]{:S(2)}, u32[]{:S(2)}) collective-permute-start(bf16[16,16,1024]{2,1,0:T(8,128)(2,1)S(1)} %get-tuple-element.157), channel_id=1, source_target_pairs={{4,0},{5,1},{6,2},{7,3},{8,4},{9,5},{10,6},{11,7},{12,8},{13,9},{1... | collective-permute-start | bytes 1572872 | tf_op jit(solution)/shard_map/ppermute | solution.py:697
  42.1 1.3 collective-permute-done.14.refs_5_
  43.6 3.4 %attend_1.1.refs_7_.after = bf16[16,112,128]{2,1,0:T(8,128)(2,1)} custom-call(s32[8,128]{1,0:T(8,128)S(1)} %make_plan.1.plan.refs_2_.requests.after, s32[8,128]{1,0:T(8,128)S(1)} %make_plan.1.plan.refs_2_.requests.after, bf16[16,8,8192]{2,1,0:T(8,128)(2,1)S(1)} %copy-done, bf16[16,8,8192]{2,1,0:T(8,128)(2,1)S(1)} %copy-done, ...), custom_call_target="tpu_custom_call", output_to_operand_aliasing={{}: (10, {})} | custom-call | tf_op jit(solution)/shard_map/attend_1/pallas_call | solution.py:136
  47.9 4.1 %collective-permute-start.19 = (bf16[16,16,1024]{2,1,0:T(8,128)(2,1)S(1)}, bf16[16,16,1024]{2,1,0:T(8,128)(2,1)}, u32[]{:S(2)}, u32[]{:S(2)}) collective-permute-start(bf16[16,16,1024]{2,1,0:T(8,128)(2,1)S(1)} %get-tuple-element.159), channel_id=1, source_target_pairs={{0,4},{1,5},{2,6},{3,7},{4,8},{5,9},{6,10},{7,11},{8,12},{9,13},{1... | collective-permute-start | bytes 1572872 | tf_op jit(solution)/shard_map/ppermute | solution.py:697
  51.9 2.0 collective-permute-start.20
  53.9 3.4 %attend_2.1.refs_9_.after = bf16[16,112,128]{2,1,0:T(8,128)(2,1)} custom-call(s32[8,128]{1,0:T(8,128)S(1)} %make_plan.1.plan.refs_2_.requests.after, s32[8,128]{1,0:T(8,128)S(1)} %make_plan.1.plan.refs_2_.requests.after, bf16[16,8,8192]{2,1,0:T(8,128)(2,1)S(1)} %copy-done, bf16[16,8,8192]{2,1,0:T(8,128)(2,1)S(1)} %copy-done, ...), custom_call_target="tpu_custom_call", output_to_operand_aliasing={{}: (10, {})} | custom-call | tf_op jit(solution)/shard_map/attend_2/pallas_call | solution.py:136
  57.6 1.9 pick_4.1
  59.5 3.0 %collective-permute-start.21 = (bf16[16,16,1024]{2,1,0:T(8,128)(2,1)S(1)}, bf16[16,16,1024]{2,1,0:T(8,128)(2,1)}, u32[]{:S(2)}, u32[]{:S(2)}) collective-permute-start(bf16[16,16,1024]{2,1,0:T(8,128)(2,1)S(1)} %get-tuple-element.161), channel_id=1, source_target_pairs={{0,4},{1,5},{2,6},{3,7},{4,8},{5,9},{6,10},{7,11},{8,12},{9,13},{1... | collective-permute-start | bytes 1572872 | tf_op jit(solution)/shard_map/ppermute | solution.py:697
  62.5 3.5 %collective-permute-start.22 = (bf16[16,16,1024]{2,1,0:T(8,128)(2,1)S(1)}, bf16[16,16,1024]{2,1,0:T(8,128)(2,1)}, u32[]{:S(2)}, u32[]{:S(2)}) collective-permute-start(bf16[16,16,1024]{2,1,0:T(8,128)(2,1)S(1)} %get-tuple-element.165), channel_id=1, source_target_pairs={{4,0},{5,1},{6,2},{7,3},{8,4},{9,5},{10,6},{11,7},{12,8},{13,9},{1... | collective-permute-start | bytes 1572872 | tf_op jit(solution)/shard_map/ppermute | solution.py:697
  66.1 1.8 collective-permute-start.23
  67.9 3.4 %attend_3.1.refs_12_ = bf16[16,112,128]{2,1,0:T(8,128)(2,1)} custom-call(s32[8,128]{1,0:T(8,128)S(1)} %make_plan.1.plan.refs_2_.requests.after, s32[8,128]{1,0:T(8,128)S(1)} %make_plan.1.plan.refs_2_.requests.after, bf16[16,8,8192]{2,1,0:T(8,128)(2,1)S(1)} %copy-done, bf16[16,8,8192]{2,1,0:T(8,128)(2,1)S(1)} %copy-done, ...), custom_call_target="tpu_custom_call", output_to_operand_aliasing={{}: (10, {})} | custom-call | tf_op jit(solution)/shard_map/attend_3/pallas_call | solution.py:136
  71.3 1.9 pick_5.1
  73.2 1.9 collective-permute-start.24
  75.1 3.5 %collective-permute-start.25 = (bf16[16,16,1024]{2,1,0:T(8,128)(2,1)S(1)}, bf16[16,16,1024]{2,1,0:T(8,128)(2,1)S(1)}, u32[]{:S(2)}, u32[]{:S(2)}) collective-permute-start(bf16[16,16,1024]{2,1,0:T(8,128)(2,1)S(1)} %get-tuple-element.168), channel_id=1, source_target_pairs={{4,0},{5,1},{6,2},{7,3},{8,4},{9,5},{10,6},{11,7},{12,8},{13,9},{1... | collective-permute-start | bytes 1572872 | tf_op jit(solution)/shard_map/ppermute | solution.py:697
  78.7 1.4 collective-permute-done.22.refs_13_
  80.1 1.9 pick_6.1
  82.0 3.0 %collective-permute-start.26 = (bf16[16,16,1024]{2,1,0:T(8,128)(2,1)S(1)}, bf16[16,16,1024]{2,1,0:T(8,128)(2,1)S(1)}, u32[]{:S(2)}, u32[]{:S(2)}) collective-permute-start(bf16[16,16,1024]{2,1,0:T(8,128)(2,1)S(1)} %get-tuple-element.169.refs_17_), channel_id=1, source_target_pairs={{0,4},{1,5},{2,6},{3,7},{4,8},{5,9},{6,10},{7,11},{8,12},{9,13},{1... | collective-permute-start | bytes 1572872 | tf_op jit(solution)/shard_map/ppermute | solution.py:697
  85.0 2.3 %collective-permute-start.27 = (bf16[16,16,1024]{2,1,0:T(8,128)(2,1)S(1)}, bf16[16,16,1024]{2,1,0:T(8,128)(2,1)S(1)}, u32[]{:S(2)}, u32[]{:S(2)}) collective-permute-start(bf16[16,16,1024]{2,1,0:T(8,128)(2,1)S(1)} %get-tuple-element.170), channel_id=1, source_target_pairs={{4,0},{5,1},{6,2},{7,3},{8,4},{9,5},{10,6},{11,7},{12,8},{13,9},{1... | collective-permute-start | bytes 1572872 | tf_op jit(solution)/shard_map/ppermute | solution.py:697
  88.5 1.1 pick_7.1
  89.6 8.4 %collective-permute-done.26.refs_17_ = bf16[16,16,1024]{2,1,0:T(8,128)(2,1)S(1)} collective-permute-done((bf16[16,16,1024]{2,1,0:T(8,128)(2,1)S(1)}, bf16[16,16,1024]{2,1,0:T(8,128)(2,1)S(1)}, u32[]{:S(2)}, u32[]{:S(2)}) %collective-permute-start.26) | collective-permute-done | bytes 524320 | tf_op jit(solution)/shard_map/ppermute | solution.py:697
  98.0 3.0 %collective-permute-done.27.refs_18_ = bf16[16,16,1024]{2,1,0:T(8,128)(2,1)S(1)} collective-permute-done((bf16[16,16,1024]{2,1,0:T(8,128)(2,1)S(1)}, bf16[16,16,1024]{2,1,0:T(8,128)(2,1)S(1)}, u32[]{:S(2)}, u32[]{:S(2)}) %collective-permute-start.27) | collective-permute-done | bytes 524320 | tf_op jit(solution)/shard_map/ppermute | solution.py:697
  102.9 8.2 %all-to-all-start.1 = ((bf16[16,112,128]{2,1,0:T(8,128)(2,1)}), bf16[16,112,128]{2,1,0:T(8,128)(2,1)S(1)}, u32[]{:S(2)}, u32[]{:S(2)}) async-start(bf16[16,112,128]{2,1,0:T(8,128)(2,1)} %attend_3.1.refs_12_), calls=%async_computation.1 | async-start | bytes 917504 | tf_op jit(solution)/shard_map/all_to_all | solution.py:725
  111.3 3.1 %collective-permute-start.29 = (bf16[16,16,1024]{2,1,0:T(8,128)(2,1)S(1)}, bf16[16,16,1024]{2,1,0:T(8,128)(2,1)}, u32[]{:S(2)}, u32[]{:S(2)}) collective-permute-start(bf16[16,16,1024]{2,1,0:T(8,128)(2,1)S(1)} %get-tuple-element.171.refs_19_), channel_id=1, source_target_pairs={{0,4},{1,5},{2,6},{3,7},{4,8},{5,9},{6,10},{7,11},{8,12},{9,13},{1... | collective-permute-start | bytes 1572872 | tf_op jit(solution)/shard_map/ppermute | solution.py:697
  114.4 3.0 %collective-permute-start.30 = (bf16[16,16,1024]{2,1,0:T(8,128)(2,1)S(1)}, bf16[16,16,1024]{2,1,0:T(8,128)(2,1)}, u32[]{:S(2)}, u32[]{:S(2)}) collective-permute-start(bf16[16,16,1024]{2,1,0:T(8,128)(2,1)S(1)} %get-tuple-element.176), channel_id=1, source_target_pairs={{4,0},{5,1},{6,2},{7,3},{8,4},{9,5},{10,6},{11,7},{12,8},{13,9},{1... | collective-permute-start | bytes 1572872 | tf_op jit(solution)/shard_map/ppermute | solution.py:697
  117.4 1.2 collective-permute-start.31
  118.6 2.3 collective-permute-start.32
  120.9 1.5 collective-permute-done.34.refs_25_
  123.2 1.9 collective-permute-start.33
  125.1 1.8 merge.1.refs_26_
  126.9 5.5 %collective-permute-done.29.refs_20_ = bf16[16,16,1024]{2,1,0:T(8,128)(2,1)} collective-permute-done((bf16[16,16,1024]{2,1,0:T(8,128)(2,1)S(1)}, bf16[16,16,1024]{2,1,0:T(8,128)(2,1)}, u32[]{:S(2)}, u32[]{:S(2)}) %collective-permute-start.29) | collective-permute-done | bytes 524320 | tf_op jit(solution)/shard_map/ppermute | solution.py:697
  132.4 1.9 collective-permute-done.30.refs_21_
  134.3 9.4 %collective-permute-done.32.refs_23_ = bf16[16,16,1024]{2,1,0:T(8,128)(2,1)S(1)} collective-permute-done((bf16[16,16,1024]{2,1,0:T(8,128)(2,1)}, bf16[16,16,1024]{2,1,0:T(8,128)(2,1)S(1)}, u32[]{:S(2)}, u32[]{:S(2)}) %collective-permute-start.32) | collective-permute-done | bytes 524320 | tf_op jit(solution)/shard_map/ppermute | solution.py:697
  146.6 2.8 %gather_give.3 = bf16[64,16,1024]{2,1,0:T(8,128)(2,1)S(1)} custom-call(s32[8,128]{1,0:T(8,128)S(1)} %make_plan.1.plan.refs_2_.requests.after, s32[2]{0:T(128)S(1)} %pad_add_fusion.place, bf16[64,16,1024]{2,1,0:T(8,128)(2,1)} %get-tuple-element.148.refs_0_, bf16[64,16,1024]{2,1,0:T(8,128)(2,1)} %collective-permute-done.10.refs_1_, ...), custom_call_target="tpu_custom_call" | custom-call | tf_op jit(solution)/shard_map/gather_give/pallas_call | solution.py:591
  152.4 3.6 %gather_own.3.cache = bf16[128,16,1024]{2,1,0:T(8,128)(2,1)} custom-call(s32[8,128]{1,0:T(8,128)S(1)} %make_plan.1.plan.refs_2_.requests.after, s32[2]{0:T(128)S(1)} %pad_add_fusion.place, bf16[64,16,1024]{2,1,0:T(8,128)(2,1)S(1)} %copy-done.4, bf16[64,16,1024]{2,1,0:T(8,128)(2,1)} %collective-permute-done.10.refs_1_, bf16[16,16,1024]{2,1,0:T(8,128)(2,1)S(1)} %copy-done.10, ...), custom_call_target="tpu_custom_call" | custom-call | tf_op jit(solution)/shard_map/gather_own/pallas_call | solution.py:628
  156.1 2.9 %fill.3 = bf16[128,16,1024]{2,1,0:T(8,128)(2,1)} custom-call(s32[2]{0:T(128)S(1)} %pad_add_fusion.place, bf16[128,16,1024]{2,1,0:T(8,128)(2,1)} %gather_own.3.cache, bf16[64,16,1024]{2,1,0:T(8,128)(2,1)} %collective-permute-done.35.other), custom_call_target="tpu_custom_call", output_to_operand_aliasing={{}: (1, {})} | custom-call | tf_op jit(solution)/shard_map/fill/pallas_call | solution.py:668
  159.0 72.3 %conditional.1 = (bf16[128,16,1024]{2,1,0:T(8,128)(2,1)}) conditional(s32[]{:T(128)} %clamp.3, bf16[128,16,1024]{2,1,0:T(8,128)(2,1)} %fill.3, (s32[8,128]{1,0:T(8,128)S(1)}, s32[2]{0:T(128)S(1)}, bf16[64,16,1024]{2,1,0:T(8,128)(2,1)}, bf16[64,16,1024]{2,1,0:T(8,128)(2,1)}, bf16[16,16,1024]{2,1,0:T(8,128)(2,1)S(1)}, ...), branch_computations={%region_0.0_spmd, %region_1.0_spmd, %region_2.8_spmd} | conditional | flops 123300 | bytes 56623820 | solution.py:757
  159.1 2.3 pick_9.1
  161.4 1.9 collective-permute-start
  163.3 3.4 %collective-permute-start.1 = (bf16[16,16,1024]{2,1,0:T(8,128)(2,1)S(1)}, bf16[16,16,1024]{2,1,0:T(8,128)(2,1)S(1)}, u32[]{:S(2)}, u32[]{:S(2)}) collective-permute-start(bf16[16,16,1024]{2,1,0:T(8,128)(2,1)S(1)} %get-tuple-element.100), channel_id=1, source_target_pairs={{4,0},{5,1},{6,2},{7,3},{8,4},{9,5},{10,6},{11,7},{12,8},{13,9},{1... | collective-permute-start | bytes 1572872 | tf_op jit(solution)/shard_map/cond/branch_1_fun/ppermute | solution.py:697
  166.8 10.7 %pick_10.1 = (bf16[16,16,1024]{2,1,0:T(8,128)(2,1)S(1)}, bf16[16,16,1024]{2,1,0:T(8,128)(2,1)S(1)}, bf16[16,16,1024]{2,1,0:T(8,128)(2,1)S(1)}) custom-call(s32[8,128]{1,0:T(8,128)S(1)} %get-tuple-element.72.plan.refs_22_, s32[2]{0:T(128)S(1)} %get-tuple-element.60.place, bf16[64,16,1024]{2,1,0:T(8,128)(2,1)S(1)} %copy-done.5, ...), custom_call_target="tpu_custom_call" | custom-call | tf_op jit(solution)/shard_map/cond/branch_1_fun/pick_10/pallas_call | solution.py:557
  177.6 1.9 collective-permute-start.3
  179.5 3.4 %collective-permute-start.4 = (bf16[16,16,1024]{2,1,0:T(8,128)(2,1)S(1)}, bf16[16,16,1024]{2,1,0:T(8,128)(2,1)S(1)}, u32[]{:S(2)}, u32[]{:S(2)}) collective-permute-start(bf16[16,16,1024]{2,1,0:T(8,128)(2,1)S(1)} %get-tuple-element.103), channel_id=1, source_target_pairs={{4,0},{5,1},{6,2},{7,3},{8,4},{9,5},{10,6},{11,7},{12,8},{13,9},{1... | collective-permute-start | bytes 1572872 | tf_op jit(solution)/shard_map/cond/branch_1_fun/ppermute | solution.py:697
  183.0 1.4 collective-permute-start.2
  184.4 1.2 pick_11.1
  185.7 1.9 collective-permute-start.6
  187.6 4.9 %collective-permute-done.3.refs_29_ = bf16[16,16,1024]{2,1,0:T(8,128)(2,1)S(1)} collective-permute-done((bf16[16,16,1024]{2,1,0:T(8,128)(2,1)S(1)}, bf16[16,16,1024]{2,1,0:T(8,128)(2,1)S(1)}, u32[]{:S(2)}, u32[]{:S(2)}) %collective-permute-start.3) | collective-permute-done | bytes 524320 | tf_op jit(solution)/shard_map/cond/branch_1_fun/ppermute | solution.py:697
  192.4 1.9 collective-permute-start.7
  195.3 11.2 %collective-permute-done.2.refs_28_ = bf16[16,16,1024]{2,1,0:T(8,128)(2,1)S(1)} collective-permute-done((bf16[16,16,1024]{2,1,0:T(8,128)(2,1)S(1)}, bf16[16,16,1024]{2,1,0:T(8,128)(2,1)S(1)}, u32[]{:S(2)}, u32[]{:S(2)}) %collective-permute-start.2) | collective-permute-done | bytes 524320 | tf_op jit(solution)/shard_map/cond/branch_1_fun/ppermute | solution.py:697
  206.6 11.2 %collective-permute-done.8.refs_34_ = bf16[16,16,1024]{2,1,0:T(8,128)(2,1)S(1)} collective-permute-done((bf16[16,16,1024]{2,1,0:T(8,128)(2,1)S(1)}, bf16[16,16,1024]{2,1,0:T(8,128)(2,1)S(1)}, u32[]{:S(2)}, u32[]{:S(2)}) %collective-permute-start.8) | collective-permute-done | bytes 524320 | tf_op jit(solution)/shard_map/cond/branch_1_fun/ppermute | solution.py:697
  217.8 4.3 %gather_give.2 = bf16[64,16,1024]{2,1,0:T(8,128)(2,1)} custom-call(s32[8,128]{1,0:T(8,128)S(1)} %get-tuple-element.72.plan.refs_22_, s32[2]{0:T(128)S(1)} %get-tuple-element.60.place, bf16[64,16,1024]{2,1,0:T(8,128)(2,1)S(1)} %copy-done.5, bf16[64,16,1024]{2,1,0:T(8,128)(2,1)} %get-tuple-element.74.refs_1_, ...), custom_call_target="tpu_custom_call" | custom-call | tf_op jit(solution)/shard_map/cond/branch_1_fun/gather_give/pallas_call | solution.py:591
  222.1 2.1 collective-permute-start.9
  224.2 3.8 %gather_own.2.cache = bf16[128,16,1024]{2,1,0:T(8,128)(2,1)} custom-call(s32[8,128]{1,0:T(8,128)S(1)} %get-tuple-element.72.plan.refs_22_, s32[2]{0:T(128)S(1)} %get-tuple-element.60.place, bf16[64,16,1024]{2,1,0:T(8,128)(2,1)S(1)} %copy-done.5, bf16[64,16,1024]{2,1,0:T(8,128)(2,1)} %get-tuple-element.74.refs_1_, ...), custom_call_target="tpu_custom_call" | custom-call | tf_op jit(solution)/shard_map/cond/branch_1_fun/gather_own/pallas_call | solution.py:628
  228.2 2.1 fill.2
  (134 shorter events, 12.9 us)
Async XLA Ops:
  0.6 8.5 %copy-start.47 = (s32[2048]{0:T(1024)S(1)}, s32[2048]{0:T(1024)}, u32[]{:S(2)}) copy-start(s32[2048]{0:T(1024)} %param.14) | copy-start | bytes 24580
  8.4 5.7 %collective-permute-start.10 = (bf16[64,16,1024]{2,1,0:T(8,128)(2,1)S(1)}, bf16[64,16,1024]{2,1,0:T(8,128)(2,1)}, u32[]{:S(2)}, u32[]{:S(2)}) collective-permute-start(bf16[64,16,1024]{2,1,0:T(8,128)(2,1)S(1)} %get-tuple-element.149), channel_id=1, source_target_pairs={{0,1},{1,0},{2,3},{3,2},{4,5},{5,4},{6,7},{7,6},{8,9},{9,8},{10,11... | collective-permute-start | bytes 6291464 | tf_op jit(solution)/shard_map/ppermute | solution.py:712
  14.1 8.2 %copy-start.3 = (bf16[64,16,1024]{2,1,0:T(8,128)(2,1)S(1)}, bf16[64,16,1024]{2,1,0:T(8,128)(2,1)}, u32[]{:S(2)}) copy-start(bf16[64,16,1024]{2,1,0:T(8,128)(2,1)} %get-tuple-element.148.refs_0_) | copy-start | bytes 6291460
  14.1 15.3 %copy-start = (bf16[16,8,8192]{2,1,0:T(8,128)(2,1)S(1)}, bf16[16,8,8192]{2,1,0:T(8,128)(2,1)}, u32[]{:S(2)}) copy-start(bf16[16,8,8192]{2,1,0:T(8,128)(2,1)} %third.7) | copy-start | bytes 6291460
  14.1 15.3 %copy-start.6 = (bf16[128,15,1024]{2,0,1:T(8,128)(2,1)S(1)}, bf16[128,15,1024]{2,0,1:T(8,128)(2,1)}, u32[]{:S(2)}) copy-start(bf16[128,15,1024]{2,0,1:T(8,128)(2,1)} %param.10) | copy-start | bytes 11796484
  14.1 15.3 %copy-start.39 = (bf16[128,1024]{1,0:T(8,128)(2,1)S(1)}, bf16[128,1024]{1,0:T(8,128)(2,1)}, u32[]{:S(2)}) copy-start(bf16[128,1024]{1,0:T(8,128)(2,1)} %val_anchor.7) | copy-start | bytes 786436
  14.2 15.3 %copy-start.46 = (f32[128,8]{0,1:T(8,128)S(1)}, f32[128,8]{0,1:T(8,128)}, u32[]{:S(2)}) copy-start(f32[128,8]{0,1:T(8,128)} %param.11) | copy-start | bytes 12292
  16.6 16.3 %collective-permute-start.11 = (bf16[16,16,1024]{2,1,0:T(8,128)(2,1)S(1)}, bf16[16,16,1024]{2,1,0:T(8,128)(2,1)S(1)}, u32[]{:S(2)}, u32[]{:S(2)}) collective-permute-start(bf16[16,16,1024]{2,1,0:T(8,128)(2,1)S(1)} %get-tuple-element.150.refs_2_), channel_id=1, source_target_pairs={{0,4},{1,5},{2,6},{3,7},{4,8},{5,9},{6,10},{7,11},{8,12},{9,13},{1... | collective-permute-start | bytes 1572872 | tf_op jit(solution)/shard_map/ppermute | solution.py:697
  19.9 15.1 %collective-permute-start.12 = (bf16[16,16,1024]{2,1,0:T(8,128)(2,1)S(1)}, bf16[16,16,1024]{2,1,0:T(8,128)(2,1)S(1)}, u32[]{:S(2)}, u32[]{:S(2)}) collective-permute-start(bf16[16,16,1024]{2,1,0:T(8,128)(2,1)S(1)} %get-tuple-element.151), channel_id=1, source_target_pairs={{4,0},{5,1},{6,2},{7,3},{8,4},{9,5},{10,6},{11,7},{12,8},{13,9},{1... | collective-permute-start | bytes 1572872 | tf_op jit(solution)/shard_map/ppermute | solution.py:697
  22.0 25.0 %collective-permute-start.13 = (bf16[24,16,1024]{2,1,0:T(8,128)(2,1)S(1)}, bf16[24,16,1024]{2,1,0:T(8,128)(2,1)S(1)}, u32[]{:S(2)}, u32[]{:S(2)}) collective-permute-start(bf16[24,16,1024]{2,1,0:T(8,128)(2,1)S(1)} %get-tuple-element.152), channel_id=1, source_target_pairs={{0,2},{1,3},{2,0},{3,1},{4,6},{5,7},{6,4},{7,5},{8,10},{9,11},{10,... | collective-permute-start | bytes 2359304 | tf_op jit(solution)/shard_map/ppermute | solution.py:697
  24.1 19.3 %collective-permute-start.14 = (bf16[16,16,1024]{2,1,0:T(8,128)(2,1)S(1)}, bf16[16,16,1024]{2,1,0:T(8,128)(2,1)S(1)}, u32[]{:S(2)}, u32[]{:S(2)}) collective-permute-start(bf16[16,16,1024]{2,1,0:T(8,128)(2,1)S(1)} %get-tuple-element.153), channel_id=1, source_target_pairs={{0,4},{1,5},{2,6},{3,7},{4,8},{5,9},{6,10},{7,11},{8,12},{9,13},{1... | collective-permute-start | bytes 1572872 | tf_op jit(solution)/shard_map/ppermute | solution.py:697
  27.2 19.8 %collective-permute-start.15 = (bf16[16,16,1024]{2,1,0:T(8,128)(2,1)S(1)}, bf16[16,16,1024]{2,1,0:T(8,128)(2,1)S(1)}, u32[]{:S(2)}, u32[]{:S(2)}) collective-permute-start(bf16[16,16,1024]{2,1,0:T(8,128)(2,1)S(1)} %get-tuple-element.154), channel_id=1, source_target_pairs={{4,0},{5,1},{6,2},{7,3},{8,4},{9,5},{10,6},{11,7},{12,8},{13,9},{1... | collective-permute-start | bytes 1572872 | tf_op jit(solution)/shard_map/ppermute | solution.py:697
  32.8 55.7 %copy-start.9 = (bf16[16,16,1024]{2,1,0:T(8,128)(2,1)}, bf16[16,16,1024]{2,1,0:T(8,128)(2,1)S(1)}, u32[]{:S(2)}) copy-start(bf16[16,16,1024]{2,1,0:T(8,128)(2,1)S(1)} %collective-permute-done.11.refs_2_) | copy-start | bytes 1572868
  35.0 53.5 %copy-start.12 = (bf16[16,16,1024]{2,1,0:T(8,128)(2,1)}, bf16[16,16,1024]{2,1,0:T(8,128)(2,1)S(1)}, u32[]{:S(2)}) copy-start(bf16[16,16,1024]{2,1,0:T(8,128)(2,1)S(1)} %collective-permute-done.12.refs_3_) | copy-start | bytes 1572868
  35.9 21.4 %collective-permute-start.16 = (bf16[16,16,1024]{2,1,0:T(8,128)(2,1)S(1)}, bf16[16,16,1024]{2,1,0:T(8,128)(2,1)}, u32[]{:S(2)}, u32[]{:S(2)}) collective-permute-start(bf16[16,16,1024]{2,1,0:T(8,128)(2,1)S(1)} %get-tuple-element.156), channel_id=1, source_target_pairs={{0,4},{1,5},{2,6},{3,7},{4,8},{5,9},{6,10},{7,11},{8,12},{9,13},{1... | collective-permute-start | bytes 1572872 | tf_op jit(solution)/shard_map/ppermute | solution.py:697
  39.0 18.6 %collective-permute-start.17 = (bf16[16,16,1024]{2,1,0:T(8,128)(2,1)S(1)}, bf16[16,16,1024]{2,1,0:T(8,128)(2,1)}, u32[]{:S(2)}, u32[]{:S(2)}) collective-permute-start(bf16[16,16,1024]{2,1,0:T(8,128)(2,1)S(1)} %get-tuple-element.157), channel_id=1, source_target_pairs={{4,0},{5,1},{6,2},{7,3},{8,4},{9,5},{10,6},{11,7},{12,8},{13,9},{1... | collective-permute-start | bytes 1572872 | tf_op jit(solution)/shard_map/ppermute | solution.py:697
  43.4 36.7 %copy-start.19 = (bf16[16,16,1024]{2,1,0:T(8,128)(2,1)}, bf16[16,16,1024]{2,1,0:T(8,128)(2,1)S(1)}, u32[]{:S(2)}) copy-start(bf16[16,16,1024]{2,1,0:T(8,128)(2,1)S(1)} %collective-permute-done.14.refs_5_) | copy-start | bytes 1572868
  43.4 27.9 %collective-permute-start.18 = (bf16[24,16,1024]{2,1,0:T(8,128)(2,1)S(1)}, bf16[24,16,1024]{2,1,0:T(8,128)(2,1)S(1)}, u32[]{:S(2)}, u32[]{:S(2)}) collective-permute-start(bf16[24,16,1024]{2,1,0:T(8,128)(2,1)S(1)} %get-tuple-element.163), channel_id=1, source_target_pairs={{0,2},{1,3},{2,0},{3,1},{4,6},{5,7},{6,4},{7,5},{8,10},{9,11},{10,... | collective-permute-start | bytes 2359304 | tf_op jit(solution)/shard_map/ppermute | solution.py:697
  47.0 24.3 %copy-start.23 = (bf16[16,16,1024]{2,1,0:T(8,128)(2,1)}, bf16[16,16,1024]{2,1,0:T(8,128)(2,1)S(1)}, u32[]{:S(2)}) copy-start(bf16[16,16,1024]{2,1,0:T(8,128)(2,1)S(1)} %collective-permute-done.15.refs_6_) | copy-start | bytes 1572868
  47.0 54.0 %copy-start.7 = (bf16[24,16,1024]{2,1,0:T(8,128)(2,1)}, bf16[24,16,1024]{2,1,0:T(8,128)(2,1)S(1)}, u32[]{:S(2)}) copy-start(bf16[24,16,1024]{2,1,0:T(8,128)(2,1)S(1)} %collective-permute-done.13.refs_4_) | copy-start | bytes 2359300
  47.9 18.2 %collective-permute-start.19 = (bf16[16,16,1024]{2,1,0:T(8,128)(2,1)S(1)}, bf16[16,16,1024]{2,1,0:T(8,128)(2,1)}, u32[]{:S(2)}, u32[]{:S(2)}) collective-permute-start(bf16[16,16,1024]{2,1,0:T(8,128)(2,1)S(1)} %get-tuple-element.159), channel_id=1, source_target_pairs={{0,4},{1,5},{2,6},{3,7},{4,8},{5,9},{6,10},{7,11},{8,12},{9,13},{1... | collective-permute-start | bytes 1572872 | tf_op jit(solution)/shard_map/ppermute | solution.py:697
  51.9 19.3 %collective-permute-start.20 = (bf16[16,16,1024]{2,1,0:T(8,128)(2,1)S(1)}, bf16[16,16,1024]{2,1,0:T(8,128)(2,1)}, u32[]{:S(2)}, u32[]{:S(2)}) collective-permute-start(bf16[16,16,1024]{2,1,0:T(8,128)(2,1)S(1)} %get-tuple-element.164), channel_id=1, source_target_pairs={{4,0},{5,1},{6,2},{7,3},{8,4},{9,5},{10,6},{11,7},{12,8},{13,9},{1... | collective-permute-start | bytes 1572872 | tf_op jit(solution)/shard_map/ppermute | solution.py:697
  59.5 19.1 %collective-permute-start.21 = (bf16[16,16,1024]{2,1,0:T(8,128)(2,1)S(1)}, bf16[16,16,1024]{2,1,0:T(8,128)(2,1)}, u32[]{:S(2)}, u32[]{:S(2)}) collective-permute-start(bf16[16,16,1024]{2,1,0:T(8,128)(2,1)S(1)} %get-tuple-element.161), channel_id=1, source_target_pairs={{0,4},{1,5},{2,6},{3,7},{4,8},{5,9},{6,10},{7,11},{8,12},{9,13},{1... | collective-permute-start | bytes 1572872 | tf_op jit(solution)/shard_map/ppermute | solution.py:697
  62.5 17.6 %collective-permute-start.22 = (bf16[16,16,1024]{2,1,0:T(8,128)(2,1)S(1)}, bf16[16,16,1024]{2,1,0:T(8,128)(2,1)}, u32[]{:S(2)}, u32[]{:S(2)}) collective-permute-start(bf16[16,16,1024]{2,1,0:T(8,128)(2,1)S(1)} %get-tuple-element.165), channel_id=1, source_target_pairs={{4,0},{5,1},{6,2},{7,3},{8,4},{9,5},{10,6},{11,7},{12,8},{13,9},{1... | collective-permute-start | bytes 1572872 | tf_op jit(solution)/shard_map/ppermute | solution.py:697
  66.1 22.4 %collective-permute-start.23 = (bf16[24,16,1024]{2,1,0:T(8,128)(2,1)S(1)}, bf16[24,16,1024]{2,1,0:T(8,128)(2,1)}, u32[]{:S(2)}, u32[]{:S(2)}) collective-permute-start(bf16[24,16,1024]{2,1,0:T(8,128)(2,1)S(1)} %get-tuple-element.166), channel_id=1, source_target_pairs={{0,2},{1,3},{2,0},{3,1},{4,6},{5,7},{6,4},{7,5},{8,10},{9,11},{10,... | collective-permute-start | bytes 2359304 | tf_op jit(solution)/shard_map/ppermute | solution.py:697
  71.3 8.8 %copy-start.15 = (bf16[24,16,1024]{2,1,0:T(8,128)(2,1)}, bf16[24,16,1024]{2,1,0:T(8,128)(2,1)S(1)}, u32[]{:S(2)}) copy-start(bf16[24,16,1024]{2,1,0:T(8,128)(2,1)S(1)} %collective-permute-done.18.refs_9_) | copy-start | bytes 2359300
  73.2 14.1 %collective-permute-start.24 = (bf16[16,16,1024]{2,1,0:T(8,128)(2,1)S(1)}, bf16[16,16,1024]{2,1,0:T(8,128)(2,1)S(1)}, u32[]{:S(2)}, u32[]{:S(2)}) collective-permute-start(bf16[16,16,1024]{2,1,0:T(8,128)(2,1)S(1)} %get-tuple-element.167.refs_14_), channel_id=1, source_target_pairs={{0,4},{1,5},{2,6},{3,7},{4,8},{5,9},{6,10},{7,11},{8,12},{9,13},{1... | collective-permute-start | bytes 1572872 | tf_op jit(solution)/shard_map/ppermute | solution.py:697
  75.1 13.4 %copy-start.24 = (bf16[16,16,1024]{2,1,0:T(8,128)(2,1)S(1)}, bf16[16,16,1024]{2,1,0:T(8,128)(2,1)}, u32[]{:S(2)}) copy-start(bf16[16,16,1024]{2,1,0:T(8,128)(2,1)} %copy-done.23) | copy-start | bytes 1572868
  75.1 13.4 %collective-permute-start.25 = (bf16[16,16,1024]{2,1,0:T(8,128)(2,1)S(1)}, bf16[16,16,1024]{2,1,0:T(8,128)(2,1)S(1)}, u32[]{:S(2)}, u32[]{:S(2)}) collective-permute-start(bf16[16,16,1024]{2,1,0:T(8,128)(2,1)S(1)} %get-tuple-element.168), channel_id=1, source_target_pairs={{4,0},{5,1},{6,2},{7,3},{8,4},{9,5},{10,6},{11,7},{12,8},{13,9},{1... | collective-permute-start | bytes 1572872 | tf_op jit(solution)/shard_map/ppermute | solution.py:697
  82.0 16.0 %collective-permute-start.26 = (bf16[16,16,1024]{2,1,0:T(8,128)(2,1)S(1)}, bf16[16,16,1024]{2,1,0:T(8,128)(2,1)S(1)}, u32[]{:S(2)}, u32[]{:S(2)}) collective-permute-start(bf16[16,16,1024]{2,1,0:T(8,128)(2,1)S(1)} %get-tuple-element.169.refs_17_), channel_id=1, source_target_pairs={{0,4},{1,5},{2,6},{3,7},{4,8},{5,9},{6,10},{7,11},{8,12},{9,13},{1... | collective-permute-start | bytes 1572872 | tf_op jit(solution)/shard_map/ppermute | solution.py:697
  85.0 16.0 %collective-permute-start.27 = (bf16[16,16,1024]{2,1,0:T(8,128)(2,1)S(1)}, bf16[16,16,1024]{2,1,0:T(8,128)(2,1)S(1)}, u32[]{:S(2)}, u32[]{:S(2)}) collective-permute-start(bf16[16,16,1024]{2,1,0:T(8,128)(2,1)S(1)} %get-tuple-element.170), channel_id=1, source_target_pairs={{4,0},{5,1},{6,2},{7,3},{8,4},{9,5},{10,6},{11,7},{12,8},{13,9},{1... | collective-permute-start | bytes 1572872 | tf_op jit(solution)/shard_map/ppermute | solution.py:697
  87.3 13.7 %copy-start.27 = (bf16[16,16,1024]{2,1,0:T(8,128)(2,1)}, bf16[16,16,1024]{2,1,0:T(8,128)(2,1)S(1)}, u32[]{:S(2)}) copy-start(bf16[16,16,1024]{2,1,0:T(8,128)(2,1)S(1)} %collective-permute-done.24.refs_15_) | copy-start | bytes 1572868
  87.4 13.7 %copy-start.16 = (bf16[24,16,1024]{2,1,0:T(8,128)(2,1)S(1)}, bf16[24,16,1024]{2,1,0:T(8,128)(2,1)}, u32[]{:S(2)}) copy-start(bf16[24,16,1024]{2,1,0:T(8,128)(2,1)} %copy-done.15) | copy-start | bytes 2359300
  87.4 13.7 %copy-start.20 = (bf16[16,16,1024]{2,1,0:T(8,128)(2,1)S(1)}, bf16[16,16,1024]{2,1,0:T(8,128)(2,1)}, u32[]{:S(2)}) copy-start(bf16[16,16,1024]{2,1,0:T(8,128)(2,1)} %copy-done.19) | copy-start | bytes 1572868
  87.4 31.2 %collective-permute-start.28 = (bf16[16,16,1024]{2,1,0:T(8,128)(2,1)S(1)}, bf16[16,16,1024]{2,1,0:T(8,128)(2,1)}, u32[]{:S(2)}, u32[]{:S(2)}) collective-permute-start(bf16[16,16,1024]{2,1,0:T(8,128)(2,1)S(1)} %get-tuple-element.175), channel_id=1, source_target_pairs={{0,2},{1,3},{2,0},{3,1},{4,6},{5,7},{6,4},{7,5},{8,10},{9,11},{10,... | collective-permute-start | bytes 1572872 | tf_op jit(solution)/shard_map/ppermute | solution.py:697
  88.5 12.5 %copy-start.30 = (bf16[16,16,1024]{2,1,0:T(8,128)(2,1)}, bf16[16,16,1024]{2,1,0:T(8,128)(2,1)S(1)}, u32[]{:S(2)}) copy-start(bf16[16,16,1024]{2,1,0:T(8,128)(2,1)S(1)} %collective-permute-done.25.refs_16_) | copy-start | bytes 1572868
  102.9 22.2 %all-to-all-start.1 = ((bf16[16,112,128]{2,1,0:T(8,128)(2,1)}), bf16[16,112,128]{2,1,0:T(8,128)(2,1)S(1)}, u32[]{:S(2)}, u32[]{:S(2)}) async-start(bf16[16,112,128]{2,1,0:T(8,128)(2,1)} %attend_3.1.refs_12_), calls=%async_computation.1 | async-start | bytes 917504 | tf_op jit(solution)/shard_map/all_to_all | solution.py:725
  111.0 11.4 %collective-permute-start.34 = (bf16[8,16,1024]{2,1,0:T(8,128)(2,1)S(1)}, bf16[8,16,1024]{2,1,0:T(8,128)(2,1)S(1)}, u32[]{:S(2)}, u32[]{:S(2)}) collective-permute-start(bf16[8,16,1024]{2,1,0:T(8,128)(2,1)S(1)} %get-tuple-element.179), channel_id=1, source_target_pairs={{0,2},{1,3},{2,0},{3,1},{4,6},{5,7},{6,4},{7,5},{8,10},{9,11},{10,... | collective-permute-start | bytes 786440 | tf_op jit(solution)/shard_map/ppermute | solution.py:697
  111.3 21.2 %collective-permute-start.29 = (bf16[16,16,1024]{2,1,0:T(8,128)(2,1)S(1)}, bf16[16,16,1024]{2,1,0:T(8,128)(2,1)}, u32[]{:S(2)}, u32[]{:S(2)}) collective-permute-start(bf16[16,16,1024]{2,1,0:T(8,128)(2,1)S(1)} %get-tuple-element.171.refs_19_), channel_id=1, source_target_pairs={{0,4},{1,5},{2,6},{3,7},{4,8},{5,9},{6,10},{7,11},{8,12},{9,13},{1... | collective-permute-start | bytes 1572872 | tf_op jit(solution)/shard_map/ppermute | solution.py:697
  114.4 20.0 %collective-permute-start.30 = (bf16[16,16,1024]{2,1,0:T(8,128)(2,1)S(1)}, bf16[16,16,1024]{2,1,0:T(8,128)(2,1)}, u32[]{:S(2)}, u32[]{:S(2)}) collective-permute-start(bf16[16,16,1024]{2,1,0:T(8,128)(2,1)S(1)} %get-tuple-element.176), channel_id=1, source_target_pairs={{4,0},{5,1},{6,2},{7,3},{8,4},{9,5},{10,6},{11,7},{12,8},{13,9},{1... | collective-permute-start | bytes 1572872 | tf_op jit(solution)/shard_map/ppermute | solution.py:697
  117.4 17.0 %collective-permute-start.31 = (bf16[16,16,1024]{2,1,0:T(8,128)(2,1)S(1)}, bf16[16,16,1024]{2,1,0:T(8,128)(2,1)}, u32[]{:S(2)}, u32[]{:S(2)}) collective-permute-start(bf16[16,16,1024]{2,1,0:T(8,128)(2,1)S(1)} %get-tuple-element.177), channel_id=1, source_target_pairs={{0,2},{1,3},{2,0},{3,1},{4,6},{5,7},{6,4},{7,5},{8,10},{9,11},{10,... | collective-permute-start | bytes 1572872 | tf_op jit(solution)/shard_map/ppermute | solution.py:697
  118.6 25.2 %collective-permute-start.32 = (bf16[16,16,1024]{2,1,0:T(8,128)(2,1)}, bf16[16,16,1024]{2,1,0:T(8,128)(2,1)S(1)}, u32[]{:S(2)}, u32[]{:S(2)}) collective-permute-start(bf16[16,16,1024]{2,1,0:T(8,128)(2,1)} %copy-done.2), channel_id=1, source_target_pairs={{0,4},{1,5},{2,6},{3,7},{4,8},{5,9},{6,10},{7,11},{8,12},{9,13},{1... | collective-permute-start | bytes 1572872 | tf_op jit(solution)/shard_map/ppermute | solution.py:697
  123.2 22.4 %collective-permute-start.33 = (bf16[16,16,1024]{2,1,0:T(8,128)(2,1)S(1)}, bf16[16,16,1024]{2,1,0:T(8,128)(2,1)}, u32[]{:S(2)}, u32[]{:S(2)}) collective-permute-start(bf16[16,16,1024]{2,1,0:T(8,128)(2,1)S(1)} %get-tuple-element.178), channel_id=1, source_target_pairs={{4,0},{5,1},{6,2},{7,3},{8,4},{9,5},{10,6},{11,7},{12,8},{13,9},{1... | collective-permute-start | bytes 1572872 | tf_op jit(solution)/shard_map/ppermute | solution.py:697
  125.1 27.2 %copy-start.10 = (bf16[16,16,1024]{2,1,0:T(8,128)(2,1)S(1)}, bf16[16,16,1024]{2,1,0:T(8,128)(2,1)}, u32[]{:S(2)}) copy-start(bf16[16,16,1024]{2,1,0:T(8,128)(2,1)} %copy-done.9) | copy-start | bytes 1572868
  149.3 6.7 %collective-permute-start.35 = (bf16[64,16,1024]{2,1,0:T(8,128)(2,1)S(1)}, bf16[64,16,1024]{2,1,0:T(8,128)(2,1)}, u32[]{:S(2)}, u32[]{:S(2)}) collective-permute-start(bf16[64,16,1024]{2,1,0:T(8,128)(2,1)S(1)} %gather_give.3), channel_id=1, source_target_pairs={{0,1},{1,0},{2,3},{3,2},{4,5},{5,4},{6,7},{7,6},{8,9},{9,8},{10,11... | collective-permute-start | bytes 6291464 | tf_op jit(solution)/shard_map/ppermute | solution.py:701
  159.0 7.7 %copy-start.5 = (bf16[64,16,1024]{2,1,0:T(8,128)(2,1)S(1)}, bf16[64,16,1024]{2,1,0:T(8,128)(2,1)}, u32[]{:S(2)}) copy-start(bf16[64,16,1024]{2,1,0:T(8,128)(2,1)} %get-tuple-element.73.refs_0_) | copy-start | bytes 6291460 | tf_op jit(solution)/shard_map/cond
  159.0 7.7 %copy-start.14 = (bf16[16,16,1024]{2,1,0:T(8,128)(2,1)S(1)}, bf16[16,16,1024]{2,1,0:T(8,128)(2,1)}, u32[]{:S(2)}) copy-start(bf16[16,16,1024]{2,1,0:T(8,128)(2,1)} %get-tuple-element.76.refs_3_) | copy-start | bytes 1572868 | tf_op jit(solution)/shard_map/cond
  159.1 7.7 %copy-start.18 = (bf16[24,16,1024]{2,1,0:T(8,128)(2,1)S(1)}, bf16[24,16,1024]{2,1,0:T(8,128)(2,1)}, u32[]{:S(2)}) copy-start(bf16[24,16,1024]{2,1,0:T(8,128)(2,1)} %get-tuple-element.82.refs_9_) | copy-start | bytes 2359300 | tf_op jit(solution)/shard_map/cond
  159.1 7.7 %copy-start.22 = (bf16[16,16,1024]{2,1,0:T(8,128)(2,1)S(1)}, bf16[16,16,1024]{2,1,0:T(8,128)(2,1)}, u32[]{:S(2)}) copy-start(bf16[16,16,1024]{2,1,0:T(8,128)(2,1)} %get-tuple-element.78.refs_5_) | copy-start | bytes 1572868 | tf_op jit(solution)/shard_map/cond
  159.1 7.7 %copy-start.26 = (bf16[16,16,1024]{2,1,0:T(8,128)(2,1)S(1)}, bf16[16,16,1024]{2,1,0:T(8,128)(2,1)}, u32[]{:S(2)}) copy-start(bf16[16,16,1024]{2,1,0:T(8,128)(2,1)} %get-tuple-element.79.refs_6_) | copy-start | bytes 1572868 | tf_op jit(solution)/shard_map/cond
  159.1 7.7 %copy-start.29 = (bf16[16,16,1024]{2,1,0:T(8,128)(2,1)S(1)}, bf16[16,16,1024]{2,1,0:T(8,128)(2,1)}, u32[]{:S(2)}) copy-start(bf16[16,16,1024]{2,1,0:T(8,128)(2,1)} %get-tuple-element.88.refs_15_) | copy-start | bytes 1572868 | tf_op jit(solution)/shard_map/cond
  159.1 7.7 %copy-start.32 = (bf16[16,16,1024]{2,1,0:T(8,128)(2,1)S(1)}, bf16[16,16,1024]{2,1,0:T(8,128)(2,1)}, u32[]{:S(2)}) copy-start(bf16[16,16,1024]{2,1,0:T(8,128)(2,1)} %get-tuple-element.89.refs_16_) | copy-start | bytes 1572868 | tf_op jit(solution)/shard_map/cond
  159.1 7.7 %copy-start.35 = (bf16[16,16,1024]{2,1,0:T(8,128)(2,1)S(1)}, bf16[16,16,1024]{2,1,0:T(8,128)(2,1)}, u32[]{:S(2)}) copy-start(bf16[16,16,1024]{2,1,0:T(8,128)(2,1)} %get-tuple-element.90.refs_17_) | copy-start | bytes 1572868 | tf_op jit(solution)/shard_map/cond
  161.4 21.6 %collective-permute-start = (bf16[16,16,1024]{2,1,0:T(8,128)(2,1)S(1)}, bf16[16,16,1024]{2,1,0:T(8,128)(2,1)S(1)}, u32[]{:S(2)}, u32[]{:S(2)}) collective-permute-start(bf16[16,16,1024]{2,1,0:T(8,128)(2,1)S(1)} %get-tuple-element.99.refs_25_), channel_id=1, source_target_pairs={{0,4},{1,5},{2,6},{3,7},{4,8},{5,9},{6,10},{7,11},{8,12},{9,13},{1... | collective-permute-start | bytes 1572872 | tf_op jit(solution)/shard_map/cond/branch_1_fun/ppermute | solution.py:697
  163.3 21.1 %collective-permute-start.1 = (bf16[16,16,1024]{2,1,0:T(8,128)(2,1)S(1)}, bf16[16,16,1024]{2,1,0:T(8,128)(2,1)S(1)}, u32[]{:S(2)}, u32[]{:S(2)}) collective-permute-start(bf16[16,16,1024]{2,1,0:T(8,128)(2,1)S(1)} %get-tuple-element.100), channel_id=1, source_target_pairs={{4,0},{5,1},{6,2},{7,3},{8,4},{9,5},{10,6},{11,7},{12,8},{13,9},{1... | collective-permute-start | bytes 1572872 | tf_op jit(solution)/shard_map/cond/branch_1_fun/ppermute | solution.py:697
  166.8 17.6 %copy-start.45 = (bf16[8,16,1024]{2,1,0:T(8,128)(2,1)S(1)}, bf16[8,16,1024]{2,1,0:T(8,128)(2,1)}, u32[]{:S(2)}) copy-start(bf16[8,16,1024]{2,1,0:T(8,128)(2,1)} %get-tuple-element.98.refs_25_) | copy-start | bytes 786436 | tf_op jit(solution)/shard_map/cond
  177.6 14.9 %collective-permute-start.3 = (bf16[16,16,1024]{2,1,0:T(8,128)(2,1)S(1)}, bf16[16,16,1024]{2,1,0:T(8,128)(2,1)S(1)}, u32[]{:S(2)}, u32[]{:S(2)}) collective-permute-start(bf16[16,16,1024]{2,1,0:T(8,128)(2,1)S(1)} %get-tuple-element.102.refs_28_), channel_id=1, source_target_pairs={{0,4},{1,5},{2,6},{3,7},{4,8},{5,9},{6,10},{7,11},{8,12},{9,13},{1... | collective-permute-start | bytes 1572872 | tf_op jit(solution)/shard_map/cond/branch_1_fun/ppermute | solution.py:697
  179.5 14.9 %collective-permute-start.4 = (bf16[16,16,1024]{2,1,0:T(8,128)(2,1)S(1)}, bf16[16,16,1024]{2,1,0:T(8,128)(2,1)S(1)}, u32[]{:S(2)}, u32[]{:S(2)}) collective-permute-start(bf16[16,16,1024]{2,1,0:T(8,128)(2,1)S(1)} %get-tuple-element.103), channel_id=1, source_target_pairs={{4,0},{5,1},{6,2},{7,3},{8,4},{9,5},{10,6},{11,7},{12,8},{13,9},{1... | collective-permute-start | bytes 1572872 | tf_op jit(solution)/shard_map/cond/branch_1_fun/ppermute | solution.py:697
  182.9 12.4 %collective-permute-start.5 = (bf16[16,16,1024]{2,1,0:T(8,128)(2,1)S(1)}, bf16[16,16,1024]{2,1,0:T(8,128)(2,1)S(1)}, u32[]{:S(2)}, u32[]{:S(2)}) collective-permute-start(bf16[16,16,1024]{2,1,0:T(8,128)(2,1)S(1)} %get-tuple-element.104), channel_id=1, source_target_pairs={{0,2},{1,3},{2,0},{3,1},{4,6},{5,7},{6,4},{7,5},{8,10},{9,11},{10,... | collective-permute-start | bytes 1572872 | tf_op jit(solution)/shard_map/cond/branch_1_fun/ppermute | solution.py:697
  183.0 23.6 %collective-permute-start.2 = (bf16[16,16,1024]{2,1,0:T(8,128)(2,1)S(1)}, bf16[16,16,1024]{2,1,0:T(8,128)(2,1)S(1)}, u32[]{:S(2)}, u32[]{:S(2)}) collective-permute-start(bf16[16,16,1024]{2,1,0:T(8,128)(2,1)S(1)} %get-tuple-element.101), channel_id=1, source_target_pairs={{0,2},{1,3},{2,0},{3,1},{4,6},{5,7},{6,4},{7,5},{8,10},{9,11},{10,... | collective-permute-start | bytes 1572872 | tf_op jit(solution)/shard_map/cond/branch_1_fun/ppermute | solution.py:697
  185.7 20.9 %collective-permute-start.6 = (bf16[16,16,1024]{2,1,0:T(8,128)(2,1)S(1)}, bf16[16,16,1024]{2,1,0:T(8,128)(2,1)S(1)}, u32[]{:S(2)}, u32[]{:S(2)}) collective-permute-start(bf16[16,16,1024]{2,1,0:T(8,128)(2,1)S(1)} %get-tuple-element.105.refs_35_), channel_id=1, source_target_pairs={{0,4},{1,5},{2,6},{3,7},{4,8},{5,9},{6,10},{7,11},{8,12},{9,13},{1... | collective-permute-start | bytes 1572872 | tf_op jit(solution)/shard_map/cond/branch_1_fun/ppermute | solution.py:697
  192.4 14.1 %collective-permute-start.7 = (bf16[16,16,1024]{2,1,0:T(8,128)(2,1)S(1)}, bf16[16,16,1024]{2,1,0:T(8,128)(2,1)S(1)}, u32[]{:S(2)}, u32[]{:S(2)}) collective-permute-start(bf16[16,16,1024]{2,1,0:T(8,128)(2,1)S(1)} %get-tuple-element.106), channel_id=1, source_target_pairs={{4,0},{5,1},{6,2},{7,3},{8,4},{9,5},{10,6},{11,7},{12,8},{13,9},{1... | collective-permute-start | bytes 1572872 | tf_op jit(solution)/shard_map/cond/branch_1_fun/ppermute | solution.py:697
  194.4 23.4 %collective-permute-start.8 = (bf16[16,16,1024]{2,1,0:T(8,128)(2,1)S(1)}, bf16[16,16,1024]{2,1,0:T(8,128)(2,1)S(1)}, u32[]{:S(2)}, u32[]{:S(2)}) collective-permute-start(bf16[16,16,1024]{2,1,0:T(8,128)(2,1)S(1)} %get-tuple-element.107), channel_id=1, source_target_pairs={{0,2},{1,3},{2,0},{3,1},{4,6},{5,7},{6,4},{7,5},{8,10},{9,11},{10,... | collective-permute-start | bytes 1572872 | tf_op jit(solution)/shard_map/cond/branch_1_fun/ppermute | solution.py:697
  222.1 6.1 %collective-permute-start.9 = (bf16[64,16,1024]{2,1,0:T(8,128)(2,1)}, bf16[64,16,1024]{2,1,0:T(8,128)(2,1)S(1)}, u32[]{:S(2)}, u32[]{:S(2)}) collective-permute-start(bf16[64,16,1024]{2,1,0:T(8,128)(2,1)} %gather_give.2), channel_id=1, source_target_pairs={{0,1},{1,0},{2,3},{3,2},{4,5},{5,4},{6,7},{7,6},{8,9},{9,8},{10,11... | collective-permute-start | bytes 6291464 | tf_op jit(solution)/shard_map/cond/branch_1_fun/ppermute | solution.py:701
  (21 other events, 97.1 us)
